TPU v7x, 32 devices: a whole 2x2x4 slice. The times are simulated.
32 devices in a mesh: dp: 16 (over z, y, core), mp: 2 (over x).
Axes of the slice: x: 2, y: 2, z: 4, core: 2. Of those that a mesh axis runs over, the one named last changes fastest.
Arguments:
- tokens_in: bfloat16 [32768, 768], P(('dp', 'mp')), may hold values from -6 to 6
- seg_lengths: int32 [64, 4], P('dp'), may hold values from 1 to 256, 512 in all within a row
- pad_counts: int32 [64], P('dp'), may hold values from 0 to 64
- w_qkv: bfloat16 [3, 768, 768], P(None, None, 'mp'), may hold values from -0.21875 to 0.21875
- qv_bias: bfloat16 [2, 768], P(None, 'mp'), may hold values from -3 to 3
- w_out: bfloat16 [768, 768], P('mp'), may hold values from -1.5 to 1.5
- out_bias: bfloat16 [768], replicated, may hold values from -3 to 3
- norm1_gain: bfloat16 [768], replicated, may hold values from 0.5 to 1.5
- norm1_bias: bfloat16 [768], replicated, may hold values from -3 to 3
- w_up: bfloat16 [768, 3072], P(None, 'mp'), may hold values from -0.21875 to 0.21875
- up_bias: bfloat16 [3072], P('mp'), may hold values from -3 to 3
- w_down: bfloat16 [3072, 768], P('mp'), may hold values from -0.109375 to 0.109375
- down_bias: bfloat16 [768], replicated, may hold values from -3 to 3
- norm2_gain: bfloat16 [768], replicated, may hold values from 0.5 to 1.5
- norm2_bias: bfloat16 [768], replicated, may hold values from -3 to 3
- cotangent: bfloat16 [32768, 768], P(('dp', 'mp')), may hold values from -6 to 6
Outputs:
- tokens_out: bfloat16 [32768, 768], P(('dp', 'mp'))
- pooled: float32 [64, 768], P(('dp', 'mp'))
- grad_input: bfloat16 [32768, 768], P(('dp', 'mp'))
- grad_qkv: float32 [3, 768, 768], P(None, None, 'mp')
- grad_qv_bias: float32 [2, 768], P(None, 'mp')
- grad_out: float32 [768, 768], P('mp')
- grad_out_bias: float32 [768], replicated
- grad_norm1_gain: float32 [768], replicated
- grad_norm1_bias: float32 [768], replicated
- grad_up: float32 [768, 3072], P(None, 'mp')
- grad_up_bias: float32 [3072], P('mp')
- grad_down: float32 [3072, 768], P('mp')
- grad_down_bias: float32 [768], replicated
- grad_norm2_gain: float32 [768], replicated
- grad_norm2_bias: float32 [768], replicated
All inputs are finite; a program needn't handle non-finite values.
Results may differ from a plain program's by a relative error of at most 0.019.
Values may be sent and summed in bfloat16 or wider, within the bound.
No kernel may reach another device: no remote copies, remote signals or barrier semaphores. Data moves between devices by JAX's collectives and lax.ppermute only.
A program may use at most 192 MiB of HBM per device.

v0:
```python
import functools

import jax
import jax.numpy as jnp
from jax import lax
from jax.experimental import pallas as pl
from jax.experimental.pallas import tpu as pltpu
from jax.sharding import PartitionSpec as P

HD = 64
SEQ = 512
PAIR = 128
EPSILON = 1e-12
SCORE_SCALE = 0.125
GELU_COEF = 0.7978845608028654
LOG2_E = 1.4426950408889634
MASKED = -1e30
F32 = jnp.float32
BF16 = jnp.bfloat16

NT = (((1,), (1,)), ((), ()))
NN = (((1,), (0,)), ((), ()))
TN = (((0,), (0,)), ((), ()))


TILE = 256
HINT = 8.0
VMEM_LIMIT = 56 * 2**20
CORE, Y, Z1, Z2 = 1, 2, 4, 8
SLOT = {CORE: 5, Y: 6, Z1: 7, Z2: 8}


def cost(gflop, size):
    return pl.CostEstimate(
        flops=int(gflop * HINT * 1e9), bytes_accessed=int(size * HINT), transcendentals=0
    )


def dot(a, b, dims=NN):
    return lax.dot_general(a, b, dims, preferred_element_type=F32)


def attn_fwd_kernel(
    info_ref, pad_ref, x_ref, w_ref, bias_ref, qa_ref, ka_ref, qkv_ref, ctx_ref, e_ref, rinv_ref
):
    limit = SEQ - pad_ref[info_ref[4] + pl.program_id(0)]
    w = jnp.concatenate([w_ref[0], w_ref[1], w_ref[2]], axis=1)
    qkv = dot(x_ref[...], w)
    bias = bias_ref[...].astype(F32)
    q = (qkv[:, :PAIR] + bias[0:1]).astype(BF16)
    k = qkv[:, PAIR : 2 * PAIR].astype(BF16)
    v = (qkv[:, 2 * PAIR :] + bias[1:2]).astype(BF16)
    qkv_ref[0], qkv_ref[1], qkv_ref[2] = q, k, v
    v_t = v.astype(F32).T.astype(BF16)
    low = lax.broadcasted_iota(jnp.int32, (SEQ, PAIR), 1) < HD
    j = lax.broadcasted_iota(jnp.int32, (64, SEQ), 0) + (SEQ - 64)
    i = lax.broadcasted_iota(jnp.int32, (64, SEQ), 1)
    seen = (j < limit) | (j == i)
    scores, weights = [], []
    for h in range(2):
        own = low if h == 0 else ~low
        scores.append(dot(jnp.where(own, k, ka_ref[0]), jnp.where(own, q, qa_ref[0]), NT))
    for h in range(2):
        tail = jnp.where(seen, scores[h][SEQ - 64 :], MASKED)
        s = jnp.concatenate([scores[h][: SEQ - 64], tail], axis=0)
        peak = jnp.max(s, axis=0, keepdims=True)
        e = jnp.exp2((s - peak) * (SCORE_SCALE * LOG2_E))
        rinv = 1.0 / jnp.sum(e, axis=0, keepdims=True)
        eb = e.astype(BF16)
        e_ref[h] = eb
        rinv_ref[0, 0, h : h + 1, :] = rinv
        weights.append((eb, rinv))
    parts = [dot(v_t[h * HD : (h + 1) * HD], e) * rinv for h, (e, rinv) in enumerate(weights)]
    ctx_ref[...] = jnp.concatenate(parts, axis=0).T.astype(BF16)


def attn_fwd(tokens, w_qkv, bias, info, pads, q_aug, k_aug, span=None, into=None):
    rows, width = tokens.shape[0] // SEQ, w_qkv.shape[2]
    pairs, model = width // PAIR, tokens.shape[1]
    first, end = span or (0, pairs)
    aug = pl.BlockSpec((1, SEQ, PAIR), lambda r, p, *_: (r, 0, 0))
    into = list(into or ())
    kernel = attn_fwd_kernel
    if into:
        kernel = lambda *refs: attn_fwd_kernel(*refs[:7], *refs[7 + len(into) :])
    return pl.pallas_call(
        kernel,
        grid_spec=pltpu.PrefetchScalarGridSpec(
            num_scalar_prefetch=2,
            grid=(rows, end - first),
            in_specs=[
                pl.BlockSpec((SEQ, model), lambda r, p, *_: (r, 0)),
                pl.BlockSpec((3, model, PAIR), lambda r, p, *_: (0, 0, first + p)),
                pl.BlockSpec((2, PAIR), lambda r, p, *_: (0, first + p)),
                aug,
                aug,
            ]
            + [pl.BlockSpec(memory_space=pl.ANY)] * len(into),
            out_specs=[
                pl.BlockSpec((3, SEQ, PAIR), lambda r, p, *_: (0, r, first + p)),
                pl.BlockSpec((SEQ, PAIR), lambda r, p, *_: (r, first + p)),
                pl.BlockSpec((2, SEQ, SEQ), lambda r, p, *_: (r * pairs + first + p, 0, 0)),
                pl.BlockSpec((1, 1, 2, SEQ), lambda r, p, *_: (r, first + p, 0, 0)),
            ],
        ),
        out_shape=[
            jax.ShapeDtypeStruct((3, rows * SEQ, width), BF16),
            jax.ShapeDtypeStruct((rows * SEQ, width), BF16),
            jax.ShapeDtypeStruct((rows * pairs * 2, SEQ, SEQ), BF16),
            jax.ShapeDtypeStruct((rows, pairs, 2, SEQ), F32),
        ],
        input_output_aliases={7 + i: i for i in range(len(into))},
        compiler_params=pltpu.CompilerParams(vmem_limit_bytes=24 * 2**20),
        cost_estimate=cost(1e-4, 1e3),
        name="attn_fwd",
    )(info, pads, tokens, w_qkv, bias, q_aug, k_aug, *into)


def attn_bwd_kernel(
    info_ref, x_ref, ga_ref, wo_ref, qkv_ref, ctx_ref, e_ref, rinv_ref,
    out_ref, own_ref, away_ref, gb_ref, acc_ref,
):
    row, last = pl.program_id(1), pl.num_programs(1) - 1
    q, k, v = qkv_ref[0], qkv_ref[1], qkv_ref[2]
    k_t = k.astype(F32).T.astype(BF16)
    d_t = dot(wo_ref[...], ga_ref[...], NT).astype(BF16).astype(F32)
    c_t = ctx_ref[...].astype(F32).T
    lane = lax.broadcasted_iota(jnp.int32, (SEQ, PAIR), 1)
    row8 = lax.broadcasted_iota(jnp.int32, (8, SEQ), 0)
    low = lane < HD
    ones = jnp.where((lane & (HD - 1)) < 2, 1.0, 0.0).astype(BF16)
    dv, dk, dq = [], [], []
    for h in range(2):
        own = low if h == 0 else ~low
        rinv = rinv_ref[0, 0, h : h + 1, :]
        mine = d_t[h * HD : (h + 1) * HD] * rinv
        minus = -jnp.sum(mine * c_t[h * HD : (h + 1) * HD], axis=0, keepdims=True)
        high = minus.astype(BF16).astype(F32)
        extra = jnp.where(row8 == 0, high, jnp.where(row8 == 1, minus - high, 0.0))
        blank = jnp.zeros((HD - 8, SEQ), F32)
        stack = [mine, extra, blank] if h == 0 else [extra, blank, mine]
        g_t = jnp.concatenate(stack, axis=0).astype(BF16)
        v_h = jnp.where(own, v, ones)
        e = e_ref[h]
        d = e * dot(v_h, g_t).astype(BF16)
        dv.append(dot(e, g_t, NT))
        dk.append(dot(d, q))
        dq.append(dot(k_t[h * HD : (h + 1) * HD], d))
    dq_t = jnp.concatenate(dq, axis=0) * SCORE_SCALE
    dk = jnp.where(low, dk[0], dk[1]) * SCORE_SCALE
    dv = jnp.where(low, dv[0], dv[1])
    dq_b = dq_t.T.astype(BF16)
    dk_b, dv_b = dk.astype(BF16), dv.astype(BF16)
    out_ref[0], out_ref[1], out_ref[2] = dq_b, dk_b, dv_b
    left = jnp.concatenate([dq_t, dk.T, dv.T], axis=0).astype(BF16)
    g_w = dot(left, x_ref[...]).reshape(3, PAIR, x_ref.shape[1])
    g_o = dot(c_t.astype(BF16), ga_ref[...])
    g_b = jnp.concatenate(
        [
            jnp.sum(dq_b.astype(F32), axis=0, keepdims=True),
            jnp.sum(dv_b.astype(F32), axis=0, keepdims=True),
        ],
        axis=0,
    )

    @pl.when(row == 0)
    def _():
        acc_ref[:3] = g_w
        acc_ref[3] = g_o
        gb_ref[...] = g_b

    @pl.when(row > 0)
    def _():
        acc_ref[:3] += g_w
        acc_ref[3] += g_o
        gb_ref[...] += g_b

    @pl.when(row == last)
    def _():
        core = info_ref[SLOT[CORE]]
        own_ref[...] = acc_ref[pl.ds(2 * core, 2)].astype(BF16)
        away_ref[...] = acc_ref[pl.ds(2 * (1 - core), 2)].astype(BF16)


def attn_bwd(info, tokens, grad_att, w_out, qkv, ctx, e, rinv):
    rows, pairs = rinv.shape[0], rinv.shape[1]
    width, model = qkv.shape[2], tokens.shape[1]
    wide = pl.BlockSpec((SEQ, model), lambda p, r, _: (r, 0))
    triple = pl.BlockSpec((3, SEQ, PAIR), lambda p, r, _: (0, r, p))
    half = pl.BlockSpec((2, PAIR, model), lambda p, r, _: (0, p, 0))
    return pl.pallas_call(
        attn_bwd_kernel,
        grid_spec=pltpu.PrefetchScalarGridSpec(
            num_scalar_prefetch=1,
            grid=(pairs, rows),
            in_specs=[
                wide,
                wide,
                pl.BlockSpec((PAIR, model), lambda p, r, _: (p, 0)),
                triple,
                pl.BlockSpec((SEQ, PAIR), lambda p, r, _: (r, p)),
                pl.BlockSpec((2, SEQ, SEQ), lambda p, r, _: (r * pairs + p, 0, 0)),
                pl.BlockSpec((1, 1, 2, SEQ), lambda p, r, _: (r, p, 0, 0)),
            ],
            out_specs=[
                triple,
                half,
                half,
                pl.BlockSpec((2, PAIR), lambda p, r, _: (0, p)),
            ],
            scratch_shapes=[pltpu.VMEM((4, PAIR, model), F32)],
        ),
        out_shape=[
            jax.ShapeDtypeStruct((3, rows * SEQ, width), BF16),
            jax.ShapeDtypeStruct((2, width, model), BF16),
            jax.ShapeDtypeStruct((2, width, model), BF16),
            jax.ShapeDtypeStruct((2, width), F32),
        ],
        compiler_params=pltpu.CompilerParams(vmem_limit_bytes=56 * 2**20),
        cost_estimate=cost(8 * rows, rows * pairs * 2 * SEQ * SEQ * 2),
        name="attn_bwd",
    )(info, tokens, grad_att, w_out, qkv, ctx, e, rinv)


def vector(x):
    return pl.BlockSpec(memory_space=pltpu.VMEM)


def normalise(v):
    centered = v - jnp.mean(v, axis=-1, keepdims=True)
    rstd = lax.rsqrt(jnp.mean(centered * centered, axis=-1, keepdims=True) + EPSILON)
    return centered * rstd, rstd


def normalise_back(dy, xhat, rstd, gain):
    dg = dy * gain
    return rstd * (
        dg
        - jnp.mean(dg, axis=-1, keepdims=True)
        - xhat * jnp.mean(dg * xhat, axis=-1, keepdims=True)
    )


def gelu_and_slope(u):
    u2 = u * u
    t = jnp.tanh(u * (GELU_COEF + (GELU_COEF * 0.044715) * u2))
    half = 0.5 + 0.5 * t
    act = u * half
    slope = half * (1.0 + u * (1.0 - t) * (GELU_COEF + (3 * GELU_COEF * 0.044715) * u2))
    return act, slope


def flat_bias(ref):
    b = ref[...].astype(F32)
    return jnp.concatenate([b[i : i + 1] for i in range(b.shape[0])], axis=1)


def by_core(core, x, ref):
    half = x.shape[1] // 2
    ref[core] = x[:, :half]
    ref[1 - core] = x[:, half:]


def units(core, mid, acc, wu_ref, ub_ref, wd_ref, act_ref, slope_ref):
    act, slope = gelu_and_slope(dot(mid, wu_ref[...]) + flat_bias(ub_ref))
    act = act.astype(BF16)
    by_core(core, act, act_ref)
    slope_ref[...] = slope.astype(BF16)
    return acc + dot(act, wd_ref[...])


def ffn_front_kernel(
    info_ref, cm_ref, co_ref, x_ref, wm_ref, wo_ref, vec_ref, wu_ref, ub_ref, wd_ref,
    mid_ref, xhat_ref, rstd_ref, part_ref, act_ref, slope_ref,
):
    vec = vec_ref[...].astype(F32)
    attended = dot(cm_ref[...], wm_ref[...]) + dot(co_ref[...], wo_ref[...])
    resid = x_ref[...].astype(F32) + (attended + vec[0:1])
    xhat, rstd = normalise(resid)
    normed = xhat * vec[1:2] + vec[2:3]
    mid = normed.astype(BF16)
    mid_ref[...] = mid
    xhat_ref[...] = xhat
    rstd_ref[...] = rstd
    part_ref[...] = units(
        info_ref[SLOT[CORE]], mid, normed + vec[3:4], wu_ref, ub_ref, wd_ref,
        act_ref, slope_ref,
    )


def halves(hidden, n=None):
    if n is None:
        return pl.BlockSpec((2, TILE, hidden // 2), lambda t, *_: (0, t, 0))
    return jax.ShapeDtypeStruct((2, n, hidden // 2), BF16)


def ffn_front(info, ctx, tokens, w_outs, vectors, w_up, up_bias, w_down):
    n, model = tokens.shape
    width, hidden = ctx[0].shape[1], w_up.shape[1]
    row = lambda c: pl.BlockSpec((TILE, c), lambda t, *_: (t, 0))
    shape = lambda c, d: jax.ShapeDtypeStruct((n, c), d)
    fixed = [vectors, w_up, up_bias, w_down]
    outs = [(model, BF16), (model, F32), (1, F32), (model, F32)]
    return pl.pallas_call(
        ffn_front_kernel,
        grid_spec=pltpu.PrefetchScalarGridSpec(
            num_scalar_prefetch=1,
            grid=(n // TILE,),
            in_specs=[row(width), row(width), row(model)] + [vector(a) for a in (*w_outs, *fixed)],
            out_specs=[row(c) for c, _ in outs] + [halves(hidden), row(hidden)],
        ),
        out_shape=[shape(*o) for o in outs] + [halves(hidden, n), shape(hidden, BF16)],
        compiler_params=pltpu.CompilerParams(vmem_limit_bytes=48 * 2**20),
        cost_estimate=cost(10, n * model * 24),
        name="ffn_front",
    )(info, *ctx, tokens, *w_outs, *fixed)


def ffn_back_kernel(
    info_ref, pad_ref, mid_ref, xhat_ref, rstd_ref, part_ref, slope_m_ref, cot_ref,
    wu_m_ref, wd_m_ref, wu_o_ref, ub_o_ref, wd_o_ref, vec_ref,
    out_ref, pool_ref, act_ref, branch_ref, um_ref, uo_ref, resid_ref, att_ref, sums_ref, ub_m_sum_ref, ub_o_sum_ref, slope_ref,
):
    t = pl.program_id(0)
    per_row = SEQ // TILE
    mid = mid_ref[...]
    core = info_ref[SLOT[CORE]]
    second = units(
        core, mid, part_ref[...], wu_o_ref, ub_o_ref, wd_o_ref, act_ref, slope_ref
    )
    vec = vec_ref[...].astype(F32)
    gain_two = vec[4:5]
    xhat_two, rstd_two = normalise(second)
    final = xhat_two * gain_two + vec[5:6]
    out_ref[...] = final.astype(BF16)
    count = SEQ - pad_ref[info_ref[4] + t // per_row]
    slot = lax.broadcasted_iota(jnp.int32, (TILE, 1), 0) + (t % per_row) * TILE
    pooled = jnp.sum(jnp.where(slot < count, final, 0.0), axis=0, keepdims=True)
    pooled = pooled / count.astype(F32)
    which = lax.broadcasted_iota(jnp.int32, pool_ref.shape, 0) == t // per_row
    pooled = jnp.where(which, pooled, 0.0)

    dy = cot_ref[...].astype(F32)
    down = lambda v: jnp.sum(v, axis=0, keepdims=True)
    sums = [down(dy * xhat_two), down(dy)]
    second_grad = normalise_back(dy, xhat_two, rstd_two, gain_two)
    branch = second_grad.astype(BF16)
    branch_ref[...] = branch
    sums.append(down(branch.astype(F32)))
    normed_grad = second_grad
    bias_sums = []
    for wu_ref, wd_ref, s_ref, up_ref in (
        (wu_o_ref, wd_o_ref, slope_ref, uo_ref),
        (wu_m_ref, wd_m_ref, slope_m_ref, um_ref),
    ):
        upper = (dot(branch, wd_ref[...], NT) * s_ref[...].astype(F32)).astype(BF16)
        by_core(core, upper, up_ref)
        bias_sums.append(down(upper.astype(F32)))
        normed_grad = normed_grad + dot(upper, wu_ref[...], NT)
    xhat_one = xhat_ref[...]
    sums += [down(normed_grad * xhat_one), down(normed_grad)]
    resid = normalise_back(normed_grad, xhat_one, rstd_ref[...], vec[1:2])
    resid_ref[...] = resid
    att = resid.astype(BF16)
    att_ref[...] = att
    sums.append(down(att.astype(F32)))
    sums = jnp.concatenate(sums, axis=0)

    @pl.when(t == 0)
    def _():
        pool_ref[...] = pooled
        sums_ref[...] = sums
        ub_o_sum_ref[...] = bias_sums[0]
        ub_m_sum_ref[...] = bias_sums[1]

    @pl.when(t > 0)
    def _():
        pool_ref[...] += pooled
        sums_ref[...] += sums
        ub_o_sum_ref[...] += bias_sums[0]
        ub_m_sum_ref[...] += bias_sums[1]


def ffn_back(info, pads, mid, xhat, rstd, part, slope, cot, w_ups, w_downs, up_bias_o, vectors):
    n, model = mid.shape
    hidden, rows = slope.shape[1], n // SEQ
    row = lambda c: pl.BlockSpec((TILE, c), lambda t, *_: (t, 0))
    keep = lambda r, c: pl.BlockSpec((r, c), lambda t, *_: (0, 0))
    shape = lambda c, d: jax.ShapeDtypeStruct((n, c), d)
    fixed = [w_ups[0], w_downs[0], w_ups[1], up_bias_o, w_downs[1], vectors]
    return pl.pallas_call(
        ffn_back_kernel,
        grid_spec=pltpu.PrefetchScalarGridSpec(
            num_scalar_prefetch=2,
            grid=(n // TILE,),
            in_specs=[row(model), row(model), row(1), row(model), row(hidden), row(model)]
            + [vector(a) for a in fixed],
            out_specs=[row(model), keep(rows, model), halves(hidden), row(model)]
            + [halves(hidden)] * 2
            + [row(model), row(model), keep(6, model), keep(1, hidden), keep(1, hidden)],
            scratch_shapes=[pltpu.VMEM((TILE, hidden), BF16)],
        ),
        out_shape=[
            shape(model, BF16),
            jax.ShapeDtypeStruct((rows, model), F32),
            halves(hidden, n),
            shape(model, BF16),
        ]
        + [halves(hidden, n)] * 2
        + [
            shape(model, F32),
            shape(model, BF16),
            jax.ShapeDtypeStruct((6, model), F32),
            jax.ShapeDtypeStruct((1, hidden), F32),
            jax.ShapeDtypeStruct((1, hidden), F32),
        ],
        compiler_params=pltpu.CompilerParams(vmem_limit_bytes=40 * 2**20),
        cost_estimate=cost(25, n * model * 40),
        name="ffn_back",
    )(info, pads, mid, xhat, rstd, part, slope, cot, *fixed)


def pack_attn_kernel(info_ref, wq_ref, wo_ref, qb_ref, attn_ref):
    r, w = wq_ref.shape[1:]
    attn_ref[:r, :w] = wq_ref[0]
    attn_ref[:r, w:] = wq_ref[1]
    attn_ref[r : r + r // 2, :w] = wq_ref[2, : r // 2]
    attn_ref[r : r + r // 2, w:] = wq_ref[2, r // 2 :]
    at = r + r // 2
    attn_ref[at : at + wo_ref.shape[0], :] = wo_ref[...]
    at += wo_ref.shape[0]
    attn_ref[at:, :] = jnp.zeros((16, 2 * w), BF16)
    attn_ref[at : at + 2, :w] = qb_ref[...]


def pack_ffn_kernel(info_ref, seg_ref, wu_ref, wd_ref, ub_ref, up_ref, down_ref, qa_ref, ka_ref):
    u, c = wu_ref.shape[0], up_ref.shape[1]
    up_ref[:u, :] = wu_ref[:, :c]
    up_ref[u : 2 * u, :] = wu_ref[:, c:]
    up_ref[2 * u :, :] = jnp.zeros((16, c), BF16)
    up_ref[2 * u : 2 * u + 2, :] = ub_ref[...]
    down_ref[...] = wd_ref[...]
    segs = seg_ref.shape[1]
    slot = lax.broadcasted_iota(jnp.int32, (SEQ, PAIR), 0)
    lane = lax.broadcasted_iota(jnp.int32, (SEQ, PAIR), 1) & (HD - 1)
    for row in range(qa_ref.shape[0]):
        end, segment = 0, jnp.zeros((SEQ, PAIR), jnp.int32)
        for s in range(segs):
            end = end + seg_ref[info_ref[4] + row, s]
            segment = segment + jnp.where(slot >= end, 1, 0)
        same = lane == segment
        ka_ref[row] = jnp.where(same & (lane < segs), 1.0, 0.0).astype(BF16)
        qa_ref[row] = jnp.where((lane < segs) & ~same, MASKED, 0.0).astype(BF16)


def pack_attn(info, w_qkv, w_out, qv_bias):
    model, width = w_qkv.shape[1:]
    out_rows = w_out.shape[0] // 4
    shape = (3 * width // 4 + out_rows + 16, model)
    whole = lambda s: pl.BlockSpec(s, lambda i, *_: (0,) * len(s))
    return pl.pallas_call(
        pack_attn_kernel,
        grid_spec=pltpu.PrefetchScalarGridSpec(
            num_scalar_prefetch=1,
            grid=(1,),
            in_specs=[
                pl.BlockSpec((3, model // 4, width), lambda i, at: (0, at[0], 0)),
                pl.BlockSpec((out_rows, model), lambda i, at: (at[0], 0)),
                whole(qv_bias.shape),
            ],
            out_specs=whole(shape),
        ),
        out_shape=jax.ShapeDtypeStruct(shape, BF16),
        cost_estimate=cost(0, 2 * 2**20),
        name="pack_attn",
    )(info, w_qkv, w_out, qv_bias)


def pack_ffn(info, rows, seg_lengths, w_up, w_down, up_bias):
    model = w_up.shape[0]
    up_rows, down_rows = model // 4, w_down.shape[0] // 4
    whole = lambda s: pl.BlockSpec(s, lambda i, *_: (0,) * len(s))
    shapes = [(2 * up_rows + 16, model), (down_rows, model)] + [(rows, SEQ, PAIR)] * 2
    return pl.pallas_call(
        pack_ffn_kernel,
        grid_spec=pltpu.PrefetchScalarGridSpec(
            num_scalar_prefetch=2,
            grid=(1,),
            in_specs=[
                pl.BlockSpec((up_rows, w_up.shape[1]), lambda i, at, _: (at[0], 0)),
                pl.BlockSpec((down_rows, model), lambda i, at, _: (at[9], 0)),
                whole(up_bias.shape),
            ],
            out_specs=[whole(s) for s in shapes],
        ),
        out_shape=[jax.ShapeDtypeStruct(s, BF16) for s in shapes],
        cost_estimate=cost(0, 4 * 2**20),
        name="pack_ffn",
    )(info, seg_lengths, w_up, w_down, up_bias)


def unpack_attn_kernel(at_ref, *refs):
    pieces, (wq_ref, wo_ref, qb_ref) = refs[:4], refs[4:]
    r, w, o = wq_ref.shape[1] // 4, wq_ref.shape[2], wo_ref.shape[0] // 4
    for i, piece in enumerate(pieces):
        q = at_ref[i]
        rows = pl.ds(pl.multiple_of(q * r, 16), r)
        wq_ref[0, rows, :] = piece[:r, :w]
        wq_ref[1, rows, :] = piece[:r, w:]
        wq_ref[2, pl.ds(pl.multiple_of(q * r, 16), r // 2), :] = piece[r : r + r // 2, :w]
        wq_ref[2, pl.ds(pl.multiple_of(q * r + r // 2, 16), r // 2), :] = piece[r : r + r // 2, w:]
        at = r + r // 2
        wo_ref[pl.ds(pl.multiple_of(q * o, 16), o), :] = piece[at : at + o, :]
    at += o
    qb_ref[...] = pieces[0][at : at + 2, :w]


def unpack_ffn_kernel(at_ref, *refs):
    ups, downs, (wu_ref, wd_ref, ub_ref) = refs[:4], refs[4:8], refs[8:]
    r, c, d = wu_ref.shape[0] // 4, wu_ref.shape[1] // 2, wd_ref.shape[0] // 4
    for i in range(4):
        rows = pl.ds(pl.multiple_of(at_ref[i] * r, 16), r)
        wu_ref[rows, :c] = ups[i][:r, :]
        wu_ref[rows, c:] = ups[i][r : 2 * r, :]
        wd_ref[pl.ds(pl.multiple_of(at_ref[9 + i] * d, 16), d), :] = downs[i][...]
    ub_ref[...] = ups[0][2 * r : 2 * r + 2, :]


def unpack(kernel, at, pieces, like):
    whole = pl.BlockSpec(memory_space=pltpu.VMEM)
    return pl.pallas_call(
        kernel,
        in_specs=[pl.BlockSpec(memory_space=pltpu.SMEM)] + [whole] * len(pieces),
        out_specs=[whole] * len(like),
        out_shape=[pltpu.VMEM(a.shape, BF16) for a in like],
        compiler_params=pltpu.CompilerParams(vmem_limit_bytes=32 * 2**20),
        cost_estimate=cost(0, 5 * 2**20),
        name=kernel.__name__,
    )(at, *pieces)


def over_mp(x):
    n = lax.axis_size("mp")
    return lax.ppermute(x, "mp", [(i, i ^ 1) for i in range(n)])


def over_dp(x, bit):
    n = lax.axis_size("dp")
    return lax.ppermute(x, "dp", [(i, i ^ bit) for i in range(n)])


def gather_pieces(rows, at_ref, refs, store):
    k = 0
    for ref in refs:
        for i in range(ref.shape[0] // rows):
            spot = pl.ds(pl.multiple_of(at_ref[k] * rows, 16), rows)
            store(spot, ref[i * rows : (i + 1) * rows, :].astype(F32))
            k += 1


def place_kernel(rows, at_ref, *refs):
    out_ref = refs[-1]

    def store(spot, value):
        out_ref[spot, :] = value

    gather_pieces(rows, at_ref, refs[:-1], store)


def place_up_kernel(rows, at_ref, *refs):
    out_ref = refs[-1]
    height, width = out_ref.shape[0], out_ref.shape[1] // 2
    k = 0
    for ref in refs[:-1]:
        for i in range(ref.shape[0] // rows):
            place, count = at_ref[k], height // rows
            spot = pl.ds(pl.multiple_of(place % count * rows, 16), rows)
            columns = pl.ds(pl.multiple_of(place // count * width, 128), width)
            out_ref[spot, columns] = ref[i * rows : (i + 1) * rows, :].astype(F32)
            k += 1


def place_attn_kernel(rows, at_ref, *refs):
    qkv_ref, out_ref, held_ref = refs[-3:]

    def store(spot, value):
        held_ref[spot, :] = value

    gather_pieces(rows, at_ref, refs[:-3], store)
    width = qkv_ref.shape[2]
    for c in range(3):
        for e in range(0, width, PAIR):
            qkv_ref[c, :, e : e + PAIR] = held_ref[c * width + e : c * width + e + PAIR, :].T
    out_ref[...] = held_ref[3 * width :, :]


def place(kernel, pieces, at, *shapes):
    total, cols = sum(piece.shape[0] for piece in pieces), pieces[0].shape[1]
    whole = pl.BlockSpec(memory_space=pltpu.VMEM)
    return pl.pallas_call(
        functools.partial(kernel, total // at.shape[0]),
        in_specs=[pl.BlockSpec(memory_space=pltpu.SMEM)] + [whole] * len(pieces),
        out_specs=[whole] * len(shapes),
        out_shape=[jax.ShapeDtypeStruct(s, F32) for s in shapes],
        scratch_shapes=[] if len(shapes) == 1 else [pltpu.VMEM((total, cols), F32)],
        compiler_params=pltpu.CompilerParams(vmem_limit_bytes=32 * 2**20),
        cost_estimate=cost(0, 6 * total * cols),
        name=kernel.__name__,
    )(at, *pieces)


def tie(x, *after):
    return lax.optimization_barrier((x,) + after)[0]


def land(info, x, got, own=None, step=None):
    n = got.shape[0]
    if own is not None:
        x = lax.dynamic_slice_in_dim(x, info[own] * n, n, 0)
    total = (x.astype(F32) + got.astype(F32)).astype(BF16)
    if step is None:
        return total
    return total, lax.dynamic_slice_in_dim(total, (1 - info[step]) * (n // 2), n // 2, 0)


def arrive(after, *flights):
    held = [c.crossed if part == "x" else c.got[part] for c, part in flights]
    held = lax.optimization_barrier((*held, after))
    for (c, part), got in zip(flights, held):
        if part == "x":
            c.crossed = got
        else:
            c.got[part] = got


class Chain:
    def __init__(self, info, bits):
        self.info, self.bits = info, bits
        self.dp_bits = [b for b in bits if b != "x"]
        self.order = [0]
        for b in reversed(self.dp_bits):
            self.order += [o ^ b for o in self.order]
        self.x, self.got, self.own, self.at = {}, {}, {}, {}
        self.held, self.back = None, list(reversed(self.dp_bits))

    def send(self, part, own, away):
        self.got[part] = over_dp(away, self.bits[0])
        self.x[part], self.own[part], self.at[part] = own, None, 0

    def hop(self, part="m", *after):
        if self.held is not None:
            return self.double(*after)
        x, at = tie(self.x[part], *after), self.at[part]
        got = self.crossed if self.bits[at] == "x" else self.got[part]
        bit = self.bits[at + 1] if at + 1 < len(self.bits) else None
        self.at[part] = at + 1
        if bit is None or bit == "x":
            x = land(self.info, x, got, self.own[part])
            self.x[part], self.own[part] = x, None
            if bit is None:
                bit = 2 * max(self.dp_bits)
                while bit < lax.axis_size("dp"):
                    x = land(self.info, x, over_dp(x, bit))
                    bit *= 2
                self.held = [x]
                self.double()
            elif part == "o":
                self.crossed = over_mp(x)
            return x
        x, away = land(self.info, x, got, self.own[part], SLOT[bit])
        self.x[part], self.own[part], self.got[part] = x, SLOT[bit], over_dp(away, bit)
        return x

    def double(self, *after):
        full = jnp.concatenate(self.held, axis=0) if len(self.held) > 1 else self.held[0]
        full = tie(full, *after)
        self.held.append(over_dp(full, self.back.pop(0)))
        return full

    def spots(self, me):
        who = me ^ jnp.array(self.order, jnp.int32)
        spot = jnp.zeros_like(who)
        for b in self.dp_bits:
            spot = 2 * spot + (who & b) // b
        return spot


def pack_small_kernel(sums_ref, um_ref, uo_ref, qm_ref, qo_ref, keep_ref, send_ref):
    n, c, w = sums_ref.shape[0], sums_ref.shape[1], qm_ref.shape[1]
    for out_ref, u_ref, q_ref in ((keep_ref, um_ref, qm_ref), (send_ref, uo_ref, qo_ref)):
        out_ref[...] = jnp.zeros(out_ref.shape, F32)
        out_ref[:n, :] = sums_ref[...]
        for i in range(u_ref.shape[1] // c):
            out_ref[n + i : n + i + 1, :] = u_ref[:, i * c : (i + 1) * c]
        at = n + u_ref.shape[1] // c
        for i in range(2):
            out_ref[at : at + 1, i * w : (i + 1) * w] = q_ref[i : i + 1, :]


def pack_small(sums, up_sums, qv_sums):
    shape = jax.ShapeDtypeStruct((16, sums.shape[1]), F32)
    return pl.pallas_call(
        pack_small_kernel, out_shape=[shape, shape], cost_estimate=cost(0, 2**18), name="pack_small"
    )(sums, *up_sums, *qv_sums)


def shards(
    tokens_in,
    seg_lengths,
    pad_counts,
    w_qkv,
    qv_bias,
    w_out,
    out_bias,
    norm1_gain,
    norm1_bias,
    w_up,
    up_bias,
    w_down,
    down_bias,
    norm2_gain,
    norm2_bias,
    cotangent,
):
    tokens, width = tokens_in.shape
    local = w_qkv.shape[2]
    me = lax.axis_index("dp")
    rows_here = tokens // SEQ
    slot = jnp.arange(13, dtype=jnp.int32)
    start = lax.axis_index("mp") * rows_here
    quarters = jnp.array([0, 2, 1, 3, 0, 0, 0, 0, 0, 0, 2, 1, 3], jnp.int32)
    quarters = quarters ^ jnp.where(slot < 4, me & 3, (me & CORE) | ((me & Z1) // 2))
    bits = jnp.where(slot == 4, start, (me >> jnp.clip(slot - 5, 0, 3)) & 1)
    info = jnp.where((slot < 4) | (slot > 8), quarters, bits)
    vectors = jnp.stack([out_bias, norm1_gain, norm1_bias, down_bias, norm2_gain, norm2_bias])
    up_bias = up_bias.reshape(-1, width)

    attn_w = pack_attn(info, w_qkv, w_out, qv_bias)
    up_w, down_w, q_aug, k_aug = pack_ffn(
        info, rows_here, seg_lengths, w_up, w_down, tie(up_bias, attn_w)
    )
    attn_w, up_w, down_w = over_mp(attn_w), over_mp(up_w), over_mp(down_w)
    early = local // PAIR - 1
    attn_args = (info, pad_counts, q_aug, k_aug)
    fwd_m = attn_fwd(tokens_in, w_qkv, qv_bias, *attn_args, span=(0, early))
    attn_w = tie(attn_w, fwd_m[1])
    attn_y, attn_core = over_dp(attn_w, Y), over_dp(attn_w, CORE)
    bias_m = tie(qv_bias, attn_w)
    fwd_m = attn_fwd(
        tokens_in, w_qkv, bias_m, *attn_args, span=(early, local // PAIR), into=fwd_m
    )
    up_w = tie(up_w, fwd_m[1])
    up_y = over_dp(up_w, Y)
    attn_core = tie(attn_core, up_w)
    attn_y = tie(attn_y, attn_core)
    w_qkv_o, w_out_o, qv_bias_o = unpack(
        unpack_attn_kernel,
        info,
        (attn_w, attn_y, attn_core, over_dp(attn_y, CORE)),
        (w_qkv, w_out, qv_bias),
    )
    w_qkvs, w_outs = (w_qkv, w_qkv_o), (w_out, w_out_o)
    fwd_o = attn_fwd(tokens_in, w_qkv_o, qv_bias_o, *attn_args)
    qkv, ctx, probs, rinv = zip(fwd_m, fwd_o)
    down_w, up_y, up_w = lax.optimization_barrier((down_w, up_y, up_w, ctx[1]))[:3]
    down_z = over_dp(down_w, Z1)
    up_core, up_both, down_core = over_dp(up_w, CORE), over_dp(up_y, CORE), over_dp(down_w, CORE)
    mid, xhat, rstd, part, act_m, slope_m = ffn_front(
        info, (ctx[0], tie(ctx[1], down_w)), tokens_in, w_outs, vectors, w_up, up_bias, w_down
    )
    down_z, up_core, up_both, down_core = lax.optimization_barrier(
        (down_z, up_core, up_both, down_core, mid)
    )[:4]
    w_up_o, w_down_o, up_bias_o = unpack(
        unpack_ffn_kernel,
        info,
        (up_w, up_y, up_core, up_both, down_w, down_z, down_core, over_dp(down_z, CORE)),
        (w_up, w_down, up_bias),
    )
    (
        tokens_out, pooled, act_o, grad_branch, upper_m, upper_o, grad_resid, grad_attended,
        sums, up_sum_m, up_sum_o,
    ) = ffn_back(
        info, pad_counts, mid, xhat, rstd, part, slope_m, cotangent, (w_up, w_up_o),
        (w_down, w_down_o), up_bias_o, vectors,
    )

    down = Chain(info, [CORE, "x", Z1, Y, Z2])
    up = Chain(info, [CORE, "x", Z1, Y, Z2])
    attn = Chain(info, [CORE, Y, "x", Z1, Z2])

    def attn_back(h, *after):
        g_att = tie(grad_attended, *after)
        dx, own, away, qv = attn_bwd(
            info, tokens_in, g_att, w_outs[h], qkv[h], ctx[h], probs[h], rinv[h]
        )
        return dx, own.reshape(-1, width), away.reshape(-1, width), qv

    def weight_grad(a, b, *after):
        return dot(tie(a, *after), b, TN).astype(BF16)

    def input_grad(h, grad_act, *after):
        return jnp.einsum(
            "cte,cde->td", tie(grad_act, *after), w_qkvs[h], preferred_element_type=F32
        )

    away = weight_grad(act_o[1], grad_branch)
    own = weight_grad(act_o[0], grad_branch, away)
    down.send("o", own, away)
    away = weight_grad(act_m[1], grad_branch, own)
    last = down.hop("o", away)
    own = weight_grad(act_m[0], grad_branch, last)
    down.send("m", own, away)
    away = weight_grad(mid, upper_o[1], own)
    own = weight_grad(mid, upper_o[0], away)
    up.send("o", own, away)
    last = down.hop("m", own)
    away = weight_grad(mid, upper_m[1], last)
    last = up.hop("o", away)
    own = weight_grad(mid, upper_m[0], last)
    up.send("m", own, away)
    dx_o, own, away, qv_o = attn_back(1, own)
    attn.send("o", own, away)
    last = up.hop("m", own)
    last = down.hop("m", last)
    last = attn.hop("o", last)
    dx_m, own, away, qv_m = attn_back(0, last)
    attn.send("m", own, away)
    small, small_send = pack_small(sums, (up_sum_m, up_sum_o), (qv_m, qv_o))
    last = down.hop("m", small)
    last = attn.hop("o", last)
    last = up.hop("m", last)
    last = attn.hop("m", last)
    small_got = over_mp(tie(small_send, last))
    count, bit = lax.axis_size("dp"), 1
    for what in "duadsaudsaudsaudsausgaupa":
        if what == "s":
            last = small = tie(small, last) + small_got
            if bit < count:
                small_got = over_dp(small, bit)
                bit *= 2
        elif what == "g":
            total = input_grad(1, dx_o, last) + grad_resid
            total = total + input_grad(0, dx_m, last)
            grad_input = last = total.astype(BF16)
        elif what == "p":
            down.held[0] = tie(down.held[0], last)
            (grad_down,) = place(place_kernel, down.held, down.spots(me), w_down.shape)
            last = grad_down
        else:
            last = {"d": down, "u": up, "a": attn}[what].hop("m", last)
    if bit > 16:
        small = small + small_got
    while bit < count:
        small = small + over_dp(small, bit)
        bit *= 2
    (grad_up,) = place(place_up_kernel, up.held, up.spots(me), w_up.shape)
    grad_qkv, grad_out = place(
        place_attn_kernel, attn.held, attn.spots(me), w_qkv.shape, w_out.shape
    )
    vectors = [small[i] for i in (5, 3, 4, 2, 0, 1)]
    grad_up_bias = small[6:8].reshape(-1)
    grad_qv_bias = small[8].reshape(2, local)
    return (
        tokens_out,
        pooled,
        grad_input,
        grad_qkv,
        grad_qv_bias,
        grad_out,
        vectors[0],
        vectors[1],
        vectors[2],
        grad_up,
        grad_up_bias,
        grad_down,
        vectors[3],
        vectors[4],
        vectors[5],
    )


def solution(mesh):
    token = P(("dp", "mp"), None)
    in_specs = (
        token,
        P("dp", None),
        P("dp"),
        P(None, None, "mp"),
        P(None, "mp"),
        P("mp", None),
        P(),
        P(),
        P(),
        P(None, "mp"),
        P("mp"),
        P("mp", None),
        P(),
        P(),
        P(),
        token,
    )
    out_specs = (
        token,
        token,
        token,
        P(None, None, "mp"),
        P(None, "mp"),
        P("mp", None),
        P(),
        P(),
        P(),
        P(None, "mp"),
        P("mp"),
        P("mp", None),
        P(),
        P(),
        P(),
    )
    return jax.shard_map(shards, mesh=mesh, in_specs=in_specs, out_specs=out_specs, check_vma=False)
```

profile of v0, /device:TPU:0, one launch (start us, length us, event | category | flops | bytes accessed | tf_op | source)
XLA Modules:
  0.0 313.7 jit_solution(11388358940781780956)
XLA Ops:
  1.8 2.6 pack_attn.1
  4.4 2.9 collective-permute-start
  8.0 3.5 %pack_ffn.1 = (bf16[400,768]{1,0:T(8,128)(2,1)}, bf16[384,768]{1,0:T(8,128)(2,1)}, bf16[2,512,128]{2,1,0:T(8,128)(2,1)}, bf16[2,512,128]{2,1,0:T(8,128)(2,1)}) custom-call(s32[13]{0:T(128)} %or_select_fusion.info_ref.refs_0_.at_ref, s32[4,4]{1,0:T(4,128)} %seg_ref.1, bf16[768,1536]{1,0:T(8,128)(2,1)} %wu_m_ref.1, bf16[1536,768]{1,0:T(8,128)(2,1)} %wd_m_ref.1, ...), custom_call_target="tpu_custom_call" | custom-call | bytes 33554432 | tf_op jit(solution)/shard_map/pack_ffn/pallas_call | solution.py:484
  13.5 7.7 %attn_fwd.3 = (bf16[3,1024,384]{2,1,0:T(8,128)(2,1)S(1)}, bf16[1024,384]{1,0:T(8,128)(2,1)S(1)}, bf16[12,512,512]{2,1,0:T(8,128)(2,1)S(1)}, f32[2,3,2,512]{3,2,1,0:T(2,128)S(1)}) custom-call(s32[13]{0:T(128)S(1)} %copy-done.17, s32[4]{0:T(128)S(1)} %copy-done.25, bf16[1024,768]{1,0:T(8,128)(2,1)S(1)} %copy-done.1, bf16[3,768,384]{2,1,0:T(8,128)(2,1)S(1)} %copy-done, ...), custom_call_target="tpu_custom_call" | custom-call | flops 800000 | bytes 8000 | tf_op jit(solution)/shard_map/attn_fwd/pallas_call | solution.py:86
  24.5 4.0 %attn_fwd.4 = (bf16[3,1024,384]{2,1,0:T(8,128)(2,1)S(1)}, bf16[1024,384]{1,0:T(8,128)(2,1)S(1)}, bf16[12,512,512]{2,1,0:T(8,128)(2,1)S(1)}, f32[2,3,2,512]{3,2,1,0:T(2,128)S(1)}) custom-call(s32[13]{0:T(128)S(1)} %copy-done.17, s32[4]{0:T(128)S(1)} %copy-done.25, ...), custom_call_target="tpu_custom_call", output_to_operand_aliasing={{0}: (7, {}), {1}: (8, {}), {2}: (9, {}), {3}: (10, {})} | custom-call | flops 800000 | bytes 8000 | tf_op jit(solution)/shard_map/attn_fwd/pallas_call | solution.py:86
  28.5 2.6 copy-done.2
  35.5 3.8 %collective-permute-done.1.refs_1_ = bf16[400,768]{1,0:T(8,128)(2,1)} collective-permute-done((bf16[400,768]{1,0:T(8,128)(2,1)}, bf16[400,768]{1,0:T(8,128)(2,1)}, u32[]{:S(2)}, u32[]{:S(2)}) %collective-permute-start.1) | collective-permute-done | bytes 614432 | tf_op jit(solution)/shard_map/ppermute | solution.py:549
  45.6 11.2 %attn_fwd.5 = (bf16[3,1024,384]{2,1,0:T(8,128)(2,1)S(1)}, bf16[1024,384]{1,0:T(8,128)(2,1)S(1)}, bf16[12,512,512]{2,1,0:T(8,128)(2,1)S(1)}, f32[2,3,2,512]{3,2,1,0:T(2,128)S(1)}) custom-call(s32[13]{0:T(128)S(1)} %copy-done.17, s32[4]{0:T(128)S(1)} %copy-done.25, bf16[1024,768]{1,0:T(8,128)(2,1)S(1)} %copy-done.1, ...), custom_call_target="tpu_custom_call" | custom-call | flops 800000 | bytes 8000 | tf_op jit(solution)/shard_map/attn_fwd/pallas_call | solution.py:86
  56.9 2.7 copy-done.26
  63.8 15.0 %ffn_front.1 = (bf16[1024,768]{1,0:T(8,128)(2,1)S(1)}, f32[1024,768]{1,0:T(8,128)}, f32[1024,1]{1,0:T(8,128)S(1)}, f32[1024,768]{1,0:T(8,128)}, bf16[2,1024,768]...) custom-call(s32[13]{0:T(128)S(1)} %copy-done.17, bf16[1024,384]{1,0:T(8,128)(2,1)S(1)} %copy-done.13, ...), custom_call_target="tpu_custom_call" | custom-call | flops 80000000000 | bytes 150994944 | tf_op jit(solution)/shard_map/ffn_front/pallas_call | solution.py:304
  84.1 39.1 %ffn_back.1 = (bf16[1024,768]{1,0:T(8,128)(2,1)}, f32[2,768]{1,0:T(2,128)}, bf16[2,1024,768]{2,1,0:T(8,128)(2,1)}, bf16[1024,768]{1,0:T(8,128)(2,1)S(1)}, bf16[2...) custom-call(s32[13]{0:T(128)S(1)} %copy-done.17, ...), custom_call_target="tpu_custom_call" | custom-call | flops 199999995904 | bytes 251658240 | tf_op jit(solution)/shard_map/ffn_back/pallas_call | solution.py:391
  123.3 2.6 slice_bitcast_fusion.2
  143.9 2.7 fusion.22
  146.6 17.6 %attn_bwd.2 = (bf16[3,1024,384]{2,1,0:T(8,128)(2,1)}, bf16[2,384,768]{2,1,0:T(8,128)(2,1)}, bf16[2,384,768]{2,1,0:T(8,128)(2,1)}, f32[2,384]{1,0:T(2,128)}) custom-call(s32[13]{0:T(128)} %or_select_fusion.info_ref.refs_0_.at_ref, bf16[1024,768]{1,0:T(8,128)(2,1)} %x_ref.9, bf16[1024,768]{1,0:T(8,128)(2,1)} %copy-done.33, bf16[384,768]{1,0:T(8,128)(2,1)} %copy-done.31, ...), custom_call_target="tpu_custom_call" | custom-call | flops 128000000000 | bytes 50331648 | tf_op jit(solution)/shard_map/attn_bwd/pallas_call | solution.py:191
  177.8 17.7 %attn_bwd.3 = (bf16[3,1024,384]{2,1,0:T(8,128)(2,1)}, bf16[2,384,768]{2,1,0:T(8,128)(2,1)}, bf16[2,384,768]{2,1,0:T(8,128)(2,1)}, f32[2,384]{1,0:T(2,128)}) custom-call(s32[13]{0:T(128)} %or_select_fusion.info_ref.refs_0_.at_ref, bf16[1024,768]{1,0:T(8,128)(2,1)} %x_ref.9, bf16[1024,768]{1,0:T(8,128)(2,1)} %copy-done.33, bf16[384,768]{1,0:T(8,128)(2,1)} %wo_ref.3, ...), custom_call_target="tpu_custom_call" | custom-call | flops 128000000000 | bytes 50331648 | tf_op jit(solution)/shard_map/attn_bwd/pallas_call | solution.py:191
  213.2 2.7 collective-permute-start.25
  215.9 10.4 %collective-permute-done.23 = bf16[384,768]{1,0:T(8,128)(2,1)S(1)} collective-permute-done((bf16[384,768]{1,0:T(8,128)(2,1)S(1)}, bf16[384,768]{1,0:T(8,128)(2,1)S(1)}, u32[]{:S(2)}, u32[]{:S(2)}) %collective-permute-start.23) | collective-permute-done | bytes 589856 | tf_op jit(solution)/shard_map/ppermute | solution.py:549
  230.6 2.4 collective-permute-start.32
  236.8 2.8 collective-permute-done.27.refs_1_
  240.1 5.6 %collective-permute-done.32 = bf16[192,768]{1,0:T(8,128)(2,1)S(1)} collective-permute-done((bf16[192,768]{1,0:T(8,128)(2,1)S(1)}, bf16[192,768]{1,0:T(8,128)(2,1)S(1)}, u32[]{:S(2)}, u32[]{:S(2)}) %collective-permute-start.32) | collective-permute-done | bytes 294944 | tf_op jit(solution)/shard_map/ppermute | solution.py:549
  249.3 2.8 collective-permute-start.36
  253.3 2.2 collective-permute-done.37
  255.8 10.3 %collective-permute-done.36.refs_1_ = bf16[96,768]{1,0:T(8,128)(2,1)S(1)} collective-permute-done((bf16[96,768]{1,0:T(8,128)(2,1)S(1)}, bf16[96,768]{1,0:T(8,128)(2,1)S(1)}, u32[]{:S(2)}, u32[]{:S(2)}) %collective-permute-start.36) | collective-permute-done | bytes 147488 | tf_op jit(solution)/shard_map/ppermute | solution.py:549
  266.4 3.3 %collective-permute-start.38 = (f32[16,768]{1,0:T(8,128)S(1)}, f32[16,768]{1,0:T(8,128)S(1)}, u32[]{:S(2)}, u32[]{:S(2)}) collective-permute-start(f32[16,768]{1,0:T(8,128)S(1)} %add.189), channel_id=1, source_target_pairs={{0,8},{2,10},{4,12},{6,14},{8,0},{10,2},{12,4},{14,6},{16,24},{18,... | collective-permute-start | bytes 147464 | tf_op jit(solution)/shard_map/ppermute | solution.py:549
  269.7 2.3 collective-permute-done.35.refs_3_
  274.0 2.8 collective-permute-start.42
  277.8 2.2 fusion.37
  280.4 3.4 %fusion = bf16[1024,768]{1,0:T(8,128)(2,1)} fusion(f32[1024,768]{1,0:T(8,128)S(1)} %copy-done.52, f32[1024,768,1]{1,0,2:T(8,128)S(1)} %fusion.37, bf16[3,1024,384]{2,1,0:T(8,128)(2,1)S(1)} %copy-done.53, bf16[3,768,384]{2,1,0:T(8,128)(2,1)S(1)} %copy-done), kind=kOutput, calls=%fused_computation.1 | convolution fusion | flops 1814298624 | bytes 11993088 | tf_op jit(solution)/shard_map/cte,cde->td/dot_general | solution.py:803
  285.9 9.6 %collective-permute-done.44.refs_3_ = bf16[384,768]{1,0:T(8,128)(2,1)S(1)} collective-permute-done((bf16[384,768]{1,0:T(8,128)(2,1)S(1)}, bf16[384,768]{1,0:T(8,128)(2,1)S(1)}, u32[]{:S(2)}, u32[]{:S(2)}) %collective-permute-start.44) | collective-permute-done | bytes 589856 | tf_op jit(solution)/shard_map/ppermute | solution.py:549
  299.9 3.0 place_kernel.1
  305.5 3.0 place_up_kernel.1
  308.6 4.7 %place_attn_kernel.1 = (f32[3,768,384]{2,1,0:T(8,128)}, f32[384,768]{1,0:T(8,128)}) custom-call(s32[16]{0:T(128)S(1)} %fusion.35.at_ref, bf16[96,768]{1,0:T(8,128)(2,1)S(1)} %add_convert_fusion.16.refs_0_, bf16[96,768]{1,0:T(8,128)(2,1)S(1)} %collective-permute-done.40.refs_1_, bf16[192,768]{1,0:T(8,128)(2,1)S(1)} %collective-permute-done.42.refs_2_, ...), custom_call_target="tpu_custom_call" | custom-call | bytes 56623104 | tf_op jit(solution)/shard_map/place_attn_kernel/pallas_call | solution.py:600
  (264 shorter events, 96.9 us)
Async XLA Ops:
  4.4 17.9 %collective-permute-start = (bf16[400,768]{1,0:T(8,128)(2,1)}, bf16[400,768]{1,0:T(8,128)(2,1)}, u32[]{:S(2)}, u32[]{:S(2)}) collective-permute-start(bf16[400,768]{1,0:T(8,128)(2,1)} %pack_attn.1), channel_id=1, source_target_pairs={{0,1},{1,0},{2,3},{3,2},{4,5},{5,4},{6,7},{7,6},{8,9},{9,8},{10,11... | collective-permute-start | bytes 1843208 | tf_op jit(solution)/shard_map/ppermute | solution.py:544
  11.5 23.2 %collective-permute-start.3 = (bf16[400,768]{1,0:T(8,128)(2,1)}, bf16[400,768]{1,0:T(8,128)(2,1)}, u32[]{:S(2)}, u32[]{:S(2)}) collective-permute-start(bf16[400,768]{1,0:T(8,128)(2,1)} %get-tuple-element.136), channel_id=1, source_target_pairs={{0,1},{1,0},{2,3},{3,2},{4,5},{5,4},{6,7},{7,6},{8,9},{9,8},{10,11... | collective-permute-start | bytes 1843208 | tf_op jit(solution)/shard_map/ppermute | solution.py:544
  22.4 12.3 %collective-permute-start.2 = (bf16[400,768]{1,0:T(8,128)(2,1)}, bf16[400,768]{1,0:T(8,128)(2,1)S(1)}, u32[]{:S(2)}, u32[]{:S(2)}) collective-permute-start(bf16[400,768]{1,0:T(8,128)(2,1)} %collective-permute-done.refs_0_), channel_id=1, source_target_pairs={{0,2},{2,0},{4,6},{6,4},{8,10},{10,8},{12,14},{14,12},{16,18},{18,... | collective-permute-start | bytes 1843208 | tf_op jit(solution)/shard_map/ppermute | solution.py:549
  22.4 16.9 %collective-permute-start.1 = (bf16[400,768]{1,0:T(8,128)(2,1)}, bf16[400,768]{1,0:T(8,128)(2,1)}, u32[]{:S(2)}, u32[]{:S(2)}) collective-permute-start(bf16[400,768]{1,0:T(8,128)(2,1)} %collective-permute-done.refs_0_), channel_id=1, source_target_pairs={{0,4},{2,6},{4,0},{6,2},{8,12},{10,14},{12,8},{14,10},{16,20},{18,... | collective-permute-start | bytes 1843208 | tf_op jit(solution)/shard_map/ppermute | solution.py:549
  39.3 22.2 %collective-permute-start.6 = (bf16[400,768]{1,0:T(8,128)(2,1)}, bf16[400,768]{1,0:T(8,128)(2,1)}, u32[]{:S(2)}, u32[]{:S(2)}) collective-permute-start(bf16[400,768]{1,0:T(8,128)(2,1)} %collective-permute-done.3.refs_0_), channel_id=1, source_target_pairs={{0,4},{2,6},{4,0},{6,2},{8,12},{10,14},{12,8},{14,10},{16,20},{18,... | collective-permute-start | bytes 1843208 | tf_op jit(solution)/shard_map/ppermute | solution.py:549
  41.0 20.5 %collective-permute-start.5 = (bf16[384,768]{1,0:T(8,128)(2,1)}, bf16[384,768]{1,0:T(8,128)(2,1)}, u32[]{:S(2)}, u32[]{:S(2)}) collective-permute-start(bf16[384,768]{1,0:T(8,128)(2,1)} %get-tuple-element.143), channel_id=1, source_target_pairs={{0,1},{1,0},{2,3},{3,2},{4,5},{5,4},{6,7},{7,6},{8,9},{9,8},{10,11... | collective-permute-start | bytes 1769480 | tf_op jit(solution)/shard_map/ppermute | solution.py:544
  61.6 17.3 %collective-permute-start.10 = (bf16[384,768]{1,0:T(8,128)(2,1)}, bf16[384,768]{1,0:T(8,128)(2,1)S(1)}, u32[]{:S(2)}, u32[]{:S(2)}) collective-permute-start(bf16[384,768]{1,0:T(8,128)(2,1)} %collective-permute-done.5.refs_4_), channel_id=1, source_target_pairs={{0,2},{2,0},{4,6},{6,4},{8,10},{10,8},{12,14},{14,12},{16,18},{18,... | collective-permute-start | bytes 1769480 | tf_op jit(solution)/shard_map/ppermute | solution.py:549
  61.6 17.2 %collective-permute-start.7 = (bf16[384,768]{1,0:T(8,128)(2,1)}, bf16[384,768]{1,0:T(8,128)(2,1)S(1)}, u32[]{:S(2)}, u32[]{:S(2)}) collective-permute-start(bf16[384,768]{1,0:T(8,128)(2,1)} %collective-permute-done.5.refs_4_), channel_id=1, source_target_pairs={{0,8},{2,10},{4,12},{6,14},{8,0},{10,2},{12,4},{14,6},{16,24},{18,... | collective-permute-start | bytes 1769480 | tf_op jit(solution)/shard_map/ppermute | solution.py:549
  63.3 15.5 %collective-permute-start.8 = (bf16[400,768]{1,0:T(8,128)(2,1)}, bf16[400,768]{1,0:T(8,128)(2,1)S(1)}, u32[]{:S(2)}, u32[]{:S(2)}) collective-permute-start(bf16[400,768]{1,0:T(8,128)(2,1)} %collective-permute-done.3.refs_0_), channel_id=1, source_target_pairs={{0,2},{2,0},{4,6},{6,4},{8,10},{10,8},{12,14},{14,12},{16,18},{18,... | collective-permute-start | bytes 1843208 | tf_op jit(solution)/shard_map/ppermute | solution.py:549
  63.4 15.4 %collective-permute-start.9 = (bf16[400,768]{1,0:T(8,128)(2,1)}, bf16[400,768]{1,0:T(8,128)(2,1)S(1)}, u32[]{:S(2)}, u32[]{:S(2)}) collective-permute-start(bf16[400,768]{1,0:T(8,128)(2,1)} %collective-permute-done.6.refs_1_), channel_id=1, source_target_pairs={{0,2},{2,0},{4,6},{6,4},{8,10},{10,8},{12,14},{14,12},{16,18},{18,... | collective-permute-start | bytes 1843208 | tf_op jit(solution)/shard_map/ppermute | solution.py:549
  141.6 26.1 %collective-permute-start.15 = (bf16[768,768]{1,0:T(8,128)(2,1)S(1)}, bf16[768,768]{1,0:T(8,128)(2,1)}, u32[]{:S(2)}, u32[]{:S(2)}) collective-permute-start(bf16[768,768]{1,0:T(8,128)(2,1)S(1)} %fusion.19), channel_id=1, source_target_pairs={{0,2},{2,0},{4,6},{6,4},{8,10},{10,8},{12,14},{14,12},{16,18},{18,... | collective-permute-start | bytes 3538952 | tf_op jit(solution)/shard_map/ppermute | solution.py:549
  141.8 29.1 %collective-permute-start.16 = (bf16[768,768]{1,0:T(8,128)(2,1)}, bf16[768,768]{1,0:T(8,128)(2,1)}, u32[]{:S(2)}, u32[]{:S(2)}) collective-permute-start(bf16[768,768]{1,0:T(8,128)(2,1)} %add_convert_fusion.7), channel_id=1, source_target_pairs={{0,1},{1,0},{2,3},{3,2},{4,5},{5,4},{6,7},{7,6},{8,9},{9,8},{10,11... | collective-permute-start | bytes 3538952 | tf_op jit(solution)/shard_map/ppermute | solution.py:544
  166.3 39.7 %collective-permute-start.20 = (bf16[768,768]{1,0:T(8,128)(2,1)}, bf16[768,768]{1,0:T(8,128)(2,1)}, u32[]{:S(2)}, u32[]{:S(2)}) collective-permute-start(bf16[768,768]{1,0:T(8,128)(2,1)} %add_convert_fusion.5), channel_id=1, source_target_pairs={{0,1},{1,0},{2,3},{3,2},{4,5},{5,4},{6,7},{7,6},{8,9},{9,8},{10,11... | collective-permute-start | bytes 3538952 | tf_op jit(solution)/shard_map/ppermute | solution.py:544
  173.6 27.4 %collective-permute-start.18 = (bf16[384,768]{1,0:T(8,128)(2,1)S(1)}, bf16[384,768]{1,0:T(8,128)(2,1)}, u32[]{:S(2)}, u32[]{:S(2)}) collective-permute-start(bf16[384,768]{1,0:T(8,128)(2,1)S(1)} %constant_dynamic-slice_fusion.9), channel_id=1, source_target_pairs={{0,8},{2,10},{4,12},{6,14},{8,0},{10,2},{12,4},{14,6},{16,24},{18,... | collective-permute-start | bytes 1769480 | tf_op jit(solution)/shard_map/ppermute | solution.py:549
  177.7 26.8 %collective-permute-start.19 = (bf16[384,768]{1,0:T(8,128)(2,1)}, bf16[384,768]{1,0:T(8,128)(2,1)}, u32[]{:S(2)}, u32[]{:S(2)}) collective-permute-start(bf16[384,768]{1,0:T(8,128)(2,1)} %constant_dynamic-slice_fusion.8), channel_id=1, source_target_pairs={{0,4},{2,6},{4,0},{6,2},{8,12},{10,14},{12,8},{14,10},{16,20},{18,... | collective-permute-start | bytes 1769480 | tf_op jit(solution)/shard_map/ppermute | solution.py:549
  195.5 13.7 %collective-permute-start.21 = (bf16[768,768]{1,0:T(8,128)(2,1)}, bf16[768,768]{1,0:T(8,128)(2,1)}, u32[]{:S(2)}, u32[]{:S(2)}) collective-permute-start(bf16[768,768]{1,0:T(8,128)(2,1)} %bitcast.68), channel_id=1, source_target_pairs={{0,2},{2,0},{4,6},{6,4},{8,10},{10,8},{12,14},{14,12},{16,18},{18,... | collective-permute-start | bytes 3538952 | tf_op jit(solution)/shard_map/ppermute | solution.py:549
  205.7 22.9 %collective-permute-start.28 = (bf16[384,768]{1,0:T(8,128)(2,1)S(1)}, bf16[384,768]{1,0:T(8,128)(2,1)S(1)}, u32[]{:S(2)}, u32[]{:S(2)}) collective-permute-start(bf16[384,768]{1,0:T(8,128)(2,1)S(1)} %add_convert_fusion.11), channel_id=1, source_target_pairs={{0,1},{1,0},{2,3},{3,2},{4,5},{5,4},{6,7},{7,6},{8,9},{9,8},{10,11... | collective-permute-start | bytes 1769480 | tf_op jit(solution)/shard_map/ppermute | solution.py:544
  207.6 18.7 %collective-permute-start.23 = (bf16[384,768]{1,0:T(8,128)(2,1)S(1)}, bf16[384,768]{1,0:T(8,128)(2,1)S(1)}, u32[]{:S(2)}, u32[]{:S(2)}) collective-permute-start(bf16[384,768]{1,0:T(8,128)(2,1)S(1)} %constant_dynamic-slice_fusion.6), channel_id=1, source_target_pairs={{0,8},{2,10},{4,12},{6,14},{8,0},{10,2},{12,4},{14,6},{16,24},{18,... | collective-permute-start | bytes 1769480 | tf_op jit(solution)/shard_map/ppermute | solution.py:549
  210.9 17.6 %collective-permute-start.26 = (f32[16,768]{1,0:T(8,128)S(1)}, f32[16,768]{1,0:T(8,128)S(1)}, u32[]{:S(2)}, u32[]{:S(2)}) collective-permute-start(f32[16,768]{1,0:T(8,128)S(1)} %copy-done.49), channel_id=1, source_target_pairs={{0,1},{1,0},{2,3},{3,2},{4,5},{5,4},{6,7},{7,6},{8,9},{9,8},{10,11... | collective-permute-start | bytes 147464 | tf_op jit(solution)/shard_map/ppermute | solution.py:544
  212.7 15.5 %collective-permute-start.24 = (bf16[384,768]{1,0:T(8,128)(2,1)S(1)}, bf16[384,768]{1,0:T(8,128)(2,1)S(1)}, u32[]{:S(2)}, u32[]{:S(2)}) collective-permute-start(bf16[384,768]{1,0:T(8,128)(2,1)S(1)} %constant_dynamic-slice_fusion.5), channel_id=1, source_target_pairs={{0,4},{2,6},{4,0},{6,2},{8,12},{10,14},{12,8},{14,10},{16,20},{18,... | collective-permute-start | bytes 1769480 | tf_op jit(solution)/shard_map/ppermute | solution.py:549
  213.2 15.2 %collective-permute-start.25 = (bf16[96,768]{1,0:T(8,128)(2,1)S(1)}, bf16[96,768]{1,0:T(8,128)(2,1)S(1)}, u32[]{:S(2)}, u32[]{:S(2)}) collective-permute-start(bf16[96,768]{1,0:T(8,128)(2,1)S(1)} %constant_dynamic-slice_fusion.4), channel_id=1, source_target_pairs={{0,16},{2,18},{4,20},{6,22},{8,24},{10,26},{12,28},{14,30},{16,0},... | collective-permute-start | bytes 442376 | tf_op jit(solution)/shard_map/ppermute | solution.py:549
  228.5 11.6 %collective-permute-start.30 = (f32[16,768]{1,0:T(8,128)S(1)}, f32[16,768]{1,0:T(8,128)S(1)}, u32[]{:S(2)}, u32[]{:S(2)}) collective-permute-start(f32[16,768]{1,0:T(8,128)S(1)} %add.181), channel_id=1, source_target_pairs={{0,2},{2,0},{4,6},{6,4},{8,10},{10,8},{12,14},{14,12},{16,18},{18,... | collective-permute-start | bytes 147464 | tf_op jit(solution)/shard_map/ppermute | solution.py:549
  228.7 10.9 %collective-permute-start.27 = (bf16[96,768]{1,0:T(8,128)(2,1)S(1)}, bf16[96,768]{1,0:T(8,128)(2,1)S(1)}, u32[]{:S(2)}, u32[]{:S(2)}) collective-permute-start(bf16[96,768]{1,0:T(8,128)(2,1)S(1)} %add_convert_fusion.18.refs_0_), channel_id=1, source_target_pairs={{0,16},{2,18},{4,20},{6,22},{8,24},{10,26},{12,28},{14,30},{16,0},... | collective-permute-start | bytes 442376 | tf_op jit(solution)/shard_map/ppermute | solution.py:549
  230.6 15.1 %collective-permute-start.32 = (bf16[192,768]{1,0:T(8,128)(2,1)S(1)}, bf16[192,768]{1,0:T(8,128)(2,1)S(1)}, u32[]{:S(2)}, u32[]{:S(2)}) collective-permute-start(bf16[192,768]{1,0:T(8,128)(2,1)S(1)} %constant_dynamic-slice_fusion.2), channel_id=1, source_target_pairs={{0,8},{2,10},{4,12},{6,14},{8,0},{10,2},{12,4},{14,6},{16,24},{18,... | collective-permute-start | bytes 884744 | tf_op jit(solution)/shard_map/ppermute | solution.py:549
  235.0 11.5 %collective-permute-start.33 = (bf16[96,768]{1,0:T(8,128)(2,1)S(1)}, bf16[96,768]{1,0:T(8,128)(2,1)S(1)}, u32[]{:S(2)}, u32[]{:S(2)}) collective-permute-start(bf16[96,768]{1,0:T(8,128)(2,1)S(1)} %constant_dynamic-slice_fusion.1), channel_id=1, source_target_pairs={{0,16},{2,18},{4,20},{6,22},{8,24},{10,26},{12,28},{14,30},{16,0},... | collective-permute-start | bytes 442376 | tf_op jit(solution)/shard_map/ppermute | solution.py:549
  247.9 24.2 %collective-permute-start.35 = (bf16[384,768]{1,0:T(8,128)(2,1)S(1)}, bf16[384,768]{1,0:T(8,128)(2,1)S(1)}, u32[]{:S(2)}, u32[]{:S(2)}) collective-permute-start(bf16[384,768]{1,0:T(8,128)(2,1)S(1)} %pad_maximum_fusion.3), channel_id=1, source_target_pairs={{0,8},{2,10},{4,12},{6,14},{8,0},{10,2},{12,4},{14,6},{16,24},{18,... | collective-permute-start | bytes 1769480 | tf_op jit(solution)/shard_map/ppermute | solution.py:549
  249.3 16.7 %collective-permute-start.36 = (bf16[96,768]{1,0:T(8,128)(2,1)S(1)}, bf16[96,768]{1,0:T(8,128)(2,1)S(1)}, u32[]{:S(2)}, u32[]{:S(2)}) collective-permute-start(bf16[96,768]{1,0:T(8,128)(2,1)S(1)} %add_convert_fusion.17.refs_0_), channel_id=1, source_target_pairs={{0,16},{2,18},{4,20},{6,22},{8,24},{10,26},{12,28},{14,30},{16,0},... | collective-permute-start | bytes 442376 | tf_op jit(solution)/shard_map/ppermute | solution.py:549
  255.5 14.1 %collective-permute-start.40 = (bf16[96,768]{1,0:T(8,128)(2,1)S(1)}, bf16[96,768]{1,0:T(8,128)(2,1)S(1)}, u32[]{:S(2)}, u32[]{:S(2)}) collective-permute-start(bf16[96,768]{1,0:T(8,128)(2,1)S(1)} %add_convert_fusion.16.refs_0_), channel_id=1, source_target_pairs={{0,16},{2,18},{4,20},{6,22},{8,24},{10,26},{12,28},{14,30},{16,0},... | collective-permute-start | bytes 442376 | tf_op jit(solution)/shard_map/ppermute | solution.py:549
  274.0 10.7 %collective-permute-start.42 = (bf16[192,768]{1,0:T(8,128)(2,1)S(1)}, bf16[192,768]{1,0:T(8,128)(2,1)S(1)}, u32[]{:S(2)}, u32[]{:S(2)}) collective-permute-start(bf16[192,768]{1,0:T(8,128)(2,1)S(1)} %pad_maximum_fusion.8), channel_id=1, source_target_pairs={{0,8},{2,10},{4,12},{6,14},{8,0},{10,2},{12,4},{14,6},{16,24},{18,... | collective-permute-start | bytes 884744 | tf_op jit(solution)/shard_map/ppermute | solution.py:549
  276.8 18.7 %collective-permute-start.44 = (bf16[384,768]{1,0:T(8,128)(2,1)S(1)}, bf16[384,768]{1,0:T(8,128)(2,1)S(1)}, u32[]{:S(2)}, u32[]{:S(2)}) collective-permute-start(bf16[384,768]{1,0:T(8,128)(2,1)S(1)} %pad_maximum_fusion.4), channel_id=1, source_target_pairs={{0,8},{2,10},{4,12},{6,14},{8,0},{10,2},{12,4},{14,6},{16,24},{18,... | collective-permute-start | bytes 1769480 | tf_op jit(solution)/shard_map/ppermute | solution.py:549
  276.9 23.0 %collective-permute-start.45 = (bf16[768,768]{1,0:T(8,128)(2,1)S(1)}, bf16[768,768]{1,0:T(8,128)(2,1)S(1)}, u32[]{:S(2)}, u32[]{:S(2)}) collective-permute-start(bf16[768,768]{1,0:T(8,128)(2,1)S(1)} %pad_maximum_fusion), channel_id=1, source_target_pairs={{0,2},{2,0},{4,6},{6,4},{8,10},{10,8},{12,14},{14,12},{16,18},{18,... | collective-permute-start | bytes 3538952 | tf_op jit(solution)/shard_map/ppermute | solution.py:549
  284.8 14.0 %collective-permute-start.43 = (bf16[384,768]{1,0:T(8,128)(2,1)S(1)}, bf16[384,768]{1,0:T(8,128)(2,1)S(1)}, u32[]{:S(2)}, u32[]{:S(2)}) collective-permute-start(bf16[384,768]{1,0:T(8,128)(2,1)S(1)} %pad_maximum_fusion.5), channel_id=1, source_target_pairs={{0,4},{2,6},{4,0},{6,2},{8,12},{10,14},{12,8},{14,10},{16,20},{18,... | collective-permute-start | bytes 1769480 | tf_op jit(solution)/shard_map/ppermute | solution.py:549
  (73 other events, 480.2 us)
where the time goes:
time: 316 us; the launch traced here: 314 us
  Pallas kernels  134 us (42%)
  waiting for transfers between devices  60.8 us (19%)
  starting transfers between devices  45.9 us (15%)
  local copies, waits for them, and re-layouts  27.3 us (9%)
  other arithmetic  19.7 us (6%)
  matrix products  18.5 us (6%)
  between operations  7.27 us (2%)
    ppermute x41, waiting for transfers between devices, over_dp(): return lax.ppermute(x, 'dp', [(i, i ^ bit) for i in range(n)])  57.6 us
    pallas_call x1, Pallas kernels, ffn_back(): pl.pallas_call(ffn_back_kernel, grid_spec=pltpu.PrefetchScalarGridSpec(nu...  39.1 us
    ppermute x41, starting transfers between devices, over_dp(): return lax.ppermute(x, 'dp', [(i, i ^ bit) for i in range(n)])  37.3 us
    pallas_call x2, Pallas kernels, attn_bwd(): pl.pallas_call(attn_bwd_kernel, grid_spec=pltpu.PrefetchScalarGridSpec(nu...  35.3 us
    pallas_call x3, Pallas kernels, attn_fwd(): pl.pallas_call(kernel, grid_spec=pltpu.PrefetchScalarGridSpec(num_scalar_...  22.9 us
    unnamed x114, local copies, waits for them, and re-layouts  19.5 us
    convert_element_type x19, other arithmetic, land(): total = (x.astype(F32) + got.astype(F32)).astype(BF16)  16.1 us
    pallas_call x1, Pallas kernels, ffn_front(): pl.pallas_call(ffn_front_kernel, grid_spec=pltpu.PrefetchScalarGridSpec(n...  15 us
  transfers between devices with their start and end apart: 48, of which 19 were waited for; matrix products, arithmetic and copies ran while one was open for 13% of the time, Pallas kernels for 27%

commit v1 on v0

--- a/solution.py
+++ b/solution.py
@@ -104,9 +104,9 @@
             ],
         ),
         out_shape=[
-            jax.ShapeDtypeStruct((3, rows * SEQ, width), BF16),
+            pltpu.HBM((3, rows * SEQ, width), BF16),
             jax.ShapeDtypeStruct((rows * SEQ, width), BF16),
-            jax.ShapeDtypeStruct((rows * pairs * 2, SEQ, SEQ), BF16),
+            pltpu.HBM((rows * pairs * 2, SEQ, SEQ), BF16),
             jax.ShapeDtypeStruct((rows, pairs, 2, SEQ), F32),
         ],
         input_output_aliases={7 + i: i for i in range(len(into))},
@@ -211,19 +211,19 @@
             scratch_shapes=[pltpu.VMEM((4, PAIR, model), F32)],
         ),
         out_shape=[
-            jax.ShapeDtypeStruct((3, rows * SEQ, width), BF16),
-            jax.ShapeDtypeStruct((2, width, model), BF16),
-            jax.ShapeDtypeStruct((2, width, model), BF16),
+            pltpu.HBM((3, rows * SEQ, width), BF16),
+            pltpu.HBM((2, width, model), BF16),
+            pltpu.HBM((2, width, model), BF16),
             jax.ShapeDtypeStruct((2, width), F32),
         ],
-        compiler_params=pltpu.CompilerParams(vmem_limit_bytes=56 * 2**20),
+        compiler_params=pltpu.CompilerParams(vmem_limit_bytes=24 * 2**20),
         cost_estimate=cost(8 * rows, rows * pairs * 2 * SEQ * SEQ * 2),
         name="attn_bwd",
-    )(info, tokens, grad_att, w_out, qkv, ctx, e, rinv)
+    )(info, tokens, grad_att, w_out, qkv, ctx, pltpu.with_memory_space_constraint(e, pltpu.HBM), rinv)
 
 
 def vector(x):
-    return pl.BlockSpec(memory_space=pltpu.VMEM)
+    return pl.BlockSpec(x.shape, lambda *_: (0,) * x.ndim)
 
 
 def normalise(v):
@@ -532,7 +532,7 @@
         kernel,
         in_specs=[pl.BlockSpec(memory_space=pltpu.SMEM)] + [whole] * len(pieces),
         out_specs=[whole] * len(like),
-        out_shape=[pltpu.VMEM(a.shape, BF16) for a in like],
+        out_shape=[jax.ShapeDtypeStruct(a.shape, BF16) for a in like],
         compiler_params=pltpu.CompilerParams(vmem_limit_bytes=32 * 2**20),
         cost_estimate=cost(0, 5 * 2**20),
         name=kernel.__name__,
@@ -833,7 +833,7 @@
     last = attn.hop("m", last)
     small_got = over_mp(tie(small_send, last))
     count, bit = lax.axis_size("dp"), 1
-    for what in "duadsaudsaudsaudsausgaupa":
+    for what in "duadsaudsaudsaudsausgauap":
         if what == "s":
             last = small = tie(small, last) + small_got
             if bit < count:

time: 316 us -> 311 us (0.984)
  local copies, waits for them, and re-layouts: 27.3 us -> 18 us
    unnamed x114 -> x130, local copies, waits for them, and re-layouts: 19.5 us -> 10 us
    pallas_call x3, Pallas kernels: 22.9 us -> 26.1 us  [attn_fwd(): pl.pallas_call(kernel, grid_spec=pltpu.PrefetchScalarGridSpec(num_scalar_...]
  transfers between devices with their start and end apart: 48 -> 48, of which waited for: 19 -> 17; matrix products, arithmetic and copies ran while one was open for 13% -> 14% of each run, Pallas kernels for 27% -> 29%
where the time goes in v1:
time: 311 us; the launch traced here: 309 us
  Pallas kernels  137 us (44%)
  waiting for transfers between devices  60.5 us (19%)
  starting transfers between devices  43.9 us (14%)
  other arithmetic  22.1 us (7%)
  matrix products  19.7 us (6%)
  local copies, waits for them, and re-layouts  18 us (6%)
  between operations  7.38 us (2%)
    ppermute x41, waiting for transfers between devices, over_dp(): return lax.ppermute(x, 'dp', [(i, i ^ bit) for i in range(n)])  56.3 us
    pallas_call x1, Pallas kernels, ffn_back(): pl.pallas_call(ffn_back_kernel, grid_spec=pltpu.PrefetchScalarGridSpec(nu...  38.8 us
    ppermute x41, starting transfers between devices, over_dp(): return lax.ppermute(x, 'dp', [(i, i ^ bit) for i in range(n)])  35.3 us
    pallas_call x2, Pallas kernels, attn_bwd(): pl.pallas_call(attn_bwd_kernel, grid_spec=pltpu.PrefetchScalarGridSpec(nu...  34 us
    pallas_call x3, Pallas kernels, attn_fwd(): pl.pallas_call(kernel, grid_spec=pltpu.PrefetchScalarGridSpec(num_scalar_...  26.1 us
    convert_element_type x19, other arithmetic, land(): total = (x.astype(F32) + got.astype(F32)).astype(BF16)  17.3 us
    pallas_call x1, Pallas kernels, ffn_front(): pl.pallas_call(ffn_front_kernel, grid_spec=pltpu.PrefetchScalarGridSpec(n...  15 us
    dot_general x8, matrix products, dot(): return lax.dot_general(a, b, dims, preferred_element_type=F32)  14.1 us
  transfers between devices with their start and end apart: 48, of which 17 were waited for; matrix products, arithmetic and copies ran while one was open for 14% of the time, Pallas kernels for 29%

profile of v1, /device:TPU:0, one launch (start us, length us, event | category | flops | bytes accessed | tf_op | source)
XLA Modules:
  0.0 308.9 jit_solution(2327726914856904947)
XLA Ops:
  1.8 2.6 pack_attn.1
  4.4 2.9 collective-permute-start
  8.0 3.5 %pack_ffn.1 = (bf16[400,768]{1,0:T(8,128)(2,1)}, bf16[384,768]{1,0:T(8,128)(2,1)}, bf16[2,512,128]{2,1,0:T(8,128)(2,1)}, bf16[2,512,128]{2,1,0:T(8,128)(2,1)}) custom-call(s32[13]{0:T(128)} %or_select_fusion.info_ref.refs_0_.at_ref, s32[4,4]{1,0:T(4,128)} %seg_ref.1, bf16[768,1536]{1,0:T(8,128)(2,1)} %wu_m_ref.1, bf16[1536,768]{1,0:T(8,128)(2,1)} %wd_m_ref.1, ...), custom_call_target="tpu_custom_call" | custom-call | bytes 33554432 | tf_op jit(solution)/shard_map/pack_ffn/pallas_call | solution.py:484
  13.5 8.8 %attn_fwd.3 = (bf16[3,1024,384]{2,1,0:T(8,128)(2,1)}, bf16[1024,384]{1,0:T(8,128)(2,1)S(1)}, bf16[12,512,512]{2,1,0:T(8,128)(2,1)}, f32[2,3,2,512]{3,2,1,0:T(2,128)S(1)}) custom-call(s32[13]{0:T(128)S(1)} %copy-done.23, s32[4]{0:T(128)S(1)} %copy-done.31, bf16[1024,768]{1,0:T(8,128)(2,1)S(1)} %copy-done.1, bf16[3,768,384]{2,1,0:T(8,128)(2,1)S(1)} %copy-done, ...), custom_call_target="tpu_custom_call" | custom-call | flops 800000 | bytes 8000 | tf_op jit(solution)/shard_map/attn_fwd/pallas_call | solution.py:86
  24.5 5.1 %attn_fwd.4 = (bf16[3,1024,384]{2,1,0:T(8,128)(2,1)}, bf16[1024,384]{1,0:T(8,128)(2,1)S(1)}, bf16[12,512,512]{2,1,0:T(8,128)(2,1)}, f32[2,3,2,512]{3,2,1,0:T(2,128)S(1)}) custom-call(s32[13]{0:T(128)S(1)} %copy-done.23, s32[4]{0:T(128)S(1)} %copy-done.31, ...), custom_call_target="tpu_custom_call", output_to_operand_aliasing={{0}: (7, {}), {1}: (8, {}), {2}: (9, {}), {3}: (10, {})} | custom-call | flops 800000 | bytes 8000 | tf_op jit(solution)/shard_map/attn_fwd/pallas_call | solution.py:86
  31.1 3.6 %collective-permute-done.3.refs_0_ = bf16[400,768]{1,0:T(8,128)(2,1)} collective-permute-done((bf16[400,768]{1,0:T(8,128)(2,1)}, bf16[400,768]{1,0:T(8,128)(2,1)}, u32[]{:S(2)}, u32[]{:S(2)}) %collective-permute-start.3) | collective-permute-done | bytes 614432 | tf_op jit(solution)/shard_map/ppermute | solution.py:544
  35.5 3.8 %collective-permute-done.1.refs_1_ = bf16[400,768]{1,0:T(8,128)(2,1)} collective-permute-done((bf16[400,768]{1,0:T(8,128)(2,1)}, bf16[400,768]{1,0:T(8,128)(2,1)}, u32[]{:S(2)}, u32[]{:S(2)}) %collective-permute-start.1) | collective-permute-done | bytes 614432 | tf_op jit(solution)/shard_map/ppermute | solution.py:549
  45.6 12.2 %attn_fwd.5 = (bf16[3,1024,384]{2,1,0:T(8,128)(2,1)}, bf16[1024,384]{1,0:T(8,128)(2,1)S(1)}, bf16[12,512,512]{2,1,0:T(8,128)(2,1)}, f32[2,3,2,512]{3,2,1,0:T(2,128)S(1)}) custom-call(s32[13]{0:T(128)S(1)} %copy-done.23, s32[4]{0:T(128)S(1)} %copy-done.31, bf16[1024,768]{1,0:T(8,128)(2,1)S(1)} %copy-done.1, ...), custom_call_target="tpu_custom_call" | custom-call | flops 800000 | bytes 8000 | tf_op jit(solution)/shard_map/attn_fwd/pallas_call | solution.py:86
  60.1 15.0 %ffn_front.1 = (bf16[1024,768]{1,0:T(8,128)(2,1)S(1)}, f32[1024,768]{1,0:T(8,128)}, f32[1024,1]{1,0:T(8,128)S(1)}, f32[1024,768]{1,0:T(8,128)}, bf16[2,1024,768]...) custom-call(s32[13]{0:T(128)S(1)} %copy-done.23, bf16[1024,384]{1,0:T(8,128)(2,1)S(1)} %copy-done.17, ...), custom_call_target="tpu_custom_call" | custom-call | flops 80000000000 | bytes 150994944 | tf_op jit(solution)/shard_map/ffn_front/pallas_call | solution.py:304
  80.4 38.8 %ffn_back.1 = (bf16[1024,768]{1,0:T(8,128)(2,1)}, f32[2,768]{1,0:T(2,128)}, bf16[2,1024,768]{2,1,0:T(8,128)(2,1)}, bf16[1024,768]{1,0:T(8,128)(2,1)S(1)}, bf16[2...) custom-call(s32[13]{0:T(128)S(1)} %copy-done.23, ...), custom_call_target="tpu_custom_call" | custom-call | flops 199999995904 | bytes 251658240 | tf_op jit(solution)/shard_map/ffn_back/pallas_call | solution.py:391
  119.2 2.6 slice_bitcast_fusion.2
  136.1 2.5 fusion.19
  140.7 2.7 fusion.22
  143.5 16.9 %attn_bwd.2 = (bf16[3,1024,384]{2,1,0:T(8,128)(2,1)}, bf16[2,384,768]{2,1,0:T(8,128)(2,1)}, bf16[2,384,768]{2,1,0:T(8,128)(2,1)}, f32[2,384]{1,0:T(2,128)S(1)}) custom-call(s32[13]{0:T(128)S(1)} %copy-done.23, bf16[1024,768]{1,0:T(8,128)(2,1)S(1)} %copy-done.2, bf16[1024,768]{1,0:T(8,128)(2,1)S(1)} %get-tuple-element.192.ga_ref, ...), custom_call_target="tpu_custom_call" | custom-call | flops 128000000000 | bytes 50331648 | tf_op jit(solution)/shard_map/attn_bwd/pallas_call | solution.py:191
  164.3 3.1 add_convert_fusion.4
  174.3 17.1 %attn_bwd.3 = (bf16[3,1024,384]{2,1,0:T(8,128)(2,1)}, bf16[2,384,768]{2,1,0:T(8,128)(2,1)}, bf16[2,384,768]{2,1,0:T(8,128)(2,1)}, f32[2,384]{1,0:T(2,128)S(1)}) custom-call(s32[13]{0:T(128)S(1)} %copy-done.23, bf16[1024,768]{1,0:T(8,128)(2,1)S(1)} %copy-done.2, bf16[1024,768]{1,0:T(8,128)(2,1)S(1)} %copy-done.40, bf16[384,768]{1,0:T(8,128)(2,1)S(1)} %copy-done.22, ...), custom_call_target="tpu_custom_call" | custom-call | flops 128000000000 | bytes 50331648 | tf_op jit(solution)/shard_map/attn_bwd/pallas_call | solution.py:191
  209.2 2.7 collective-permute-start.25
  211.8 10.7 %collective-permute-done.23 = bf16[384,768]{1,0:T(8,128)(2,1)S(1)} collective-permute-done((bf16[384,768]{1,0:T(8,128)(2,1)S(1)}, bf16[384,768]{1,0:T(8,128)(2,1)S(1)}, u32[]{:S(2)}, u32[]{:S(2)}) %collective-permute-start.23) | collective-permute-done | bytes 589856 | tf_op jit(solution)/shard_map/ppermute | solution.py:549
  226.3 2.5 collective-permute-start.32
  228.8 2.1 collective-permute-done.29
  232.2 3.6 %collective-permute-done.27.refs_1_ = bf16[96,768]{1,0:T(8,128)(2,1)S(1)} collective-permute-done((bf16[96,768]{1,0:T(8,128)(2,1)S(1)}, bf16[96,768]{1,0:T(8,128)(2,1)S(1)}, u32[]{:S(2)}, u32[]{:S(2)}) %collective-permute-start.27) | collective-permute-done | bytes 147488 | tf_op jit(solution)/shard_map/ppermute | solution.py:549
  236.3 5.6 %collective-permute-done.32 = bf16[192,768]{1,0:T(8,128)(2,1)S(1)} collective-permute-done((bf16[192,768]{1,0:T(8,128)(2,1)S(1)}, bf16[192,768]{1,0:T(8,128)(2,1)S(1)}, u32[]{:S(2)}, u32[]{:S(2)}) %collective-permute-start.32) | collective-permute-done | bytes 294944 | tf_op jit(solution)/shard_map/ppermute | solution.py:549
  249.0 2.2 collective-permute-done.37
  251.5 10.5 %collective-permute-done.36.refs_1_ = bf16[96,768]{1,0:T(8,128)(2,1)S(1)} collective-permute-done((bf16[96,768]{1,0:T(8,128)(2,1)S(1)}, bf16[96,768]{1,0:T(8,128)(2,1)S(1)}, u32[]{:S(2)}, u32[]{:S(2)}) %collective-permute-start.36) | collective-permute-done | bytes 147488 | tf_op jit(solution)/shard_map/ppermute | solution.py:549
  263.0 3.0 collective-permute-start.38
  270.6 2.3 collective-permute-start.42
  274.2 2.2 fusion.37
  276.8 3.4 %fusion = bf16[1024,768]{1,0:T(8,128)(2,1)} fusion(f32[1024,768]{1,0:T(8,128)S(1)} %copy-done.60, f32[1024,768,1]{1,0,2:T(8,128)S(1)} %fusion.37, bf16[3,1024,384]{2,1,0:T(8,128)(2,1)S(1)} %copy-done.61, bf16[3,768,384]{2,1,0:T(8,128)(2,1)S(1)} %copy-done), kind=kOutput, calls=%fused_computation.1 | convolution fusion | flops 1814298624 | bytes 11993088 | tf_op jit(solution)/shard_map/cte,cde->td/dot_general | solution.py:803
  281.8 9.5 %collective-permute-done.44.refs_3_ = bf16[384,768]{1,0:T(8,128)(2,1)S(1)} collective-permute-done((bf16[384,768]{1,0:T(8,128)(2,1)S(1)}, bf16[384,768]{1,0:T(8,128)(2,1)S(1)}, u32[]{:S(2)}, u32[]{:S(2)}) %collective-permute-start.44) | collective-permute-done | bytes 589856 | tf_op jit(solution)/shard_map/ppermute | solution.py:549
  296.1 3.8 %place_kernel.1 = f32[1536,768]{1,0:T(8,128)} custom-call(s32[16]{0:T(128)S(1)} %fusion.34.at_ref, bf16[96,768]{1,0:T(8,128)(2,1)S(1)} %add_convert_fusion.18.refs_0_, bf16[96,768]{1,0:T(8,128)(2,1)S(1)} %collective-permute-done.27.refs_1_, bf16[192,768]{1,0:T(8,128)(2,1)S(1)} %collective-permute-done.31.refs_2_, bf16[384,768]{1,0:T(8,128)(2,1)S(1)} %copy-done.5, ...), custom_call_target="tpu_custom_call" | custom-call | bytes 56623104 | tf_op jit(solution)/shard_map/place_kernel/pallas_call | solution.py:600
  299.9 3.8 %place_up_kernel.1 = f32[768,1536]{1,0:T(8,128)} custom-call(s32[16]{0:T(128)S(1)} %fusion.34.at_ref, bf16[96,768]{1,0:T(8,128)(2,1)S(1)} %add_convert_fusion.17.refs_0_, bf16[96,768]{1,0:T(8,128)(2,1)S(1)} %collective-permute-done.36.refs_1_, bf16[192,768]{1,0:T(8,128)(2,1)S(1)} %collective-permute-done.39.refs_2_, bf16[384,768]{1,0:T(8,128)(2,1)S(1)} %copy-done.7, ...), custom_call_target="tpu_custom_call" | custom-call | bytes 56623104 | tf_op jit(solution)/shard_map/place_up_kernel/pallas_call | solution.py:600
  303.7 4.7 %place_attn_kernel.1 = (f32[3,768,384]{2,1,0:T(8,128)}, f32[384,768]{1,0:T(8,128)}) custom-call(s32[16]{0:T(128)S(1)} %fusion.35.at_ref, bf16[96,768]{1,0:T(8,128)(2,1)S(1)} %add_convert_fusion.16.refs_0_, bf16[96,768]{1,0:T(8,128)(2,1)S(1)} %collective-permute-done.40.refs_1_, bf16[192,768]{1,0:T(8,128)(2,1)S(1)} %collective-permute-done.42.refs_2_, ...), custom_call_target="tpu_custom_call" | custom-call | bytes 56623104 | tf_op jit(solution)/shard_map/place_attn_kernel/pallas_call | solution.py:600
  (280 shorter events, 87.6 us)
Async XLA Ops:
  4.4 17.9 %collective-permute-start = (bf16[400,768]{1,0:T(8,128)(2,1)}, bf16[400,768]{1,0:T(8,128)(2,1)}, u32[]{:S(2)}, u32[]{:S(2)}) collective-permute-start(bf16[400,768]{1,0:T(8,128)(2,1)} %pack_attn.1), channel_id=1, source_target_pairs={{0,1},{1,0},{2,3},{3,2},{4,5},{5,4},{6,7},{7,6},{8,9},{9,8},{10,11... | collective-permute-start | bytes 1843208 | tf_op jit(solution)/shard_map/ppermute | solution.py:544
  11.5 23.2 %collective-permute-start.3 = (bf16[400,768]{1,0:T(8,128)(2,1)}, bf16[400,768]{1,0:T(8,128)(2,1)}, u32[]{:S(2)}, u32[]{:S(2)}) collective-permute-start(bf16[400,768]{1,0:T(8,128)(2,1)} %get-tuple-element.136), channel_id=1, source_target_pairs={{0,1},{1,0},{2,3},{3,2},{4,5},{5,4},{6,7},{7,6},{8,9},{9,8},{10,11... | collective-permute-start | bytes 1843208 | tf_op jit(solution)/shard_map/ppermute | solution.py:544
  22.4 12.3 %collective-permute-start.2 = (bf16[400,768]{1,0:T(8,128)(2,1)}, bf16[400,768]{1,0:T(8,128)(2,1)S(1)}, u32[]{:S(2)}, u32[]{:S(2)}) collective-permute-start(bf16[400,768]{1,0:T(8,128)(2,1)} %collective-permute-done.refs_0_), channel_id=1, source_target_pairs={{0,2},{2,0},{4,6},{6,4},{8,10},{10,8},{12,14},{14,12},{16,18},{18,... | collective-permute-start | bytes 1843208 | tf_op jit(solution)/shard_map/ppermute | solution.py:549
  22.4 16.9 %collective-permute-start.1 = (bf16[400,768]{1,0:T(8,128)(2,1)}, bf16[400,768]{1,0:T(8,128)(2,1)}, u32[]{:S(2)}, u32[]{:S(2)}) collective-permute-start(bf16[400,768]{1,0:T(8,128)(2,1)} %collective-permute-done.refs_0_), channel_id=1, source_target_pairs={{0,4},{2,6},{4,0},{6,2},{8,12},{10,14},{12,8},{14,10},{16,20},{18,... | collective-permute-start | bytes 1843208 | tf_op jit(solution)/shard_map/ppermute | solution.py:549
  39.3 18.5 %collective-permute-start.6 = (bf16[400,768]{1,0:T(8,128)(2,1)}, bf16[400,768]{1,0:T(8,128)(2,1)}, u32[]{:S(2)}, u32[]{:S(2)}) collective-permute-start(bf16[400,768]{1,0:T(8,128)(2,1)} %collective-permute-done.3.refs_0_), channel_id=1, source_target_pairs={{0,4},{2,6},{4,0},{6,2},{8,12},{10,14},{12,8},{14,10},{16,20},{18,... | collective-permute-start | bytes 1843208 | tf_op jit(solution)/shard_map/ppermute | solution.py:549
  41.0 16.8 %collective-permute-start.5 = (bf16[384,768]{1,0:T(8,128)(2,1)}, bf16[384,768]{1,0:T(8,128)(2,1)}, u32[]{:S(2)}, u32[]{:S(2)}) collective-permute-start(bf16[384,768]{1,0:T(8,128)(2,1)} %get-tuple-element.143), channel_id=1, source_target_pairs={{0,1},{1,0},{2,3},{3,2},{4,5},{5,4},{6,7},{7,6},{8,9},{9,8},{10,11... | collective-permute-start | bytes 1769480 | tf_op jit(solution)/shard_map/ppermute | solution.py:544
  57.9 17.2 %collective-permute-start.10 = (bf16[384,768]{1,0:T(8,128)(2,1)}, bf16[384,768]{1,0:T(8,128)(2,1)S(1)}, u32[]{:S(2)}, u32[]{:S(2)}) collective-permute-start(bf16[384,768]{1,0:T(8,128)(2,1)} %collective-permute-done.5.refs_4_), channel_id=1, source_target_pairs={{0,2},{2,0},{4,6},{6,4},{8,10},{10,8},{12,14},{14,12},{16,18},{18,... | collective-permute-start | bytes 1769480 | tf_op jit(solution)/shard_map/ppermute | solution.py:549
  57.9 17.1 %collective-permute-start.7 = (bf16[384,768]{1,0:T(8,128)(2,1)}, bf16[384,768]{1,0:T(8,128)(2,1)S(1)}, u32[]{:S(2)}, u32[]{:S(2)}) collective-permute-start(bf16[384,768]{1,0:T(8,128)(2,1)} %collective-permute-done.5.refs_4_), channel_id=1, source_target_pairs={{0,8},{2,10},{4,12},{6,14},{8,0},{10,2},{12,4},{14,6},{16,24},{18,... | collective-permute-start | bytes 1769480 | tf_op jit(solution)/shard_map/ppermute | solution.py:549
  59.6 15.5 %collective-permute-start.8 = (bf16[400,768]{1,0:T(8,128)(2,1)}, bf16[400,768]{1,0:T(8,128)(2,1)S(1)}, u32[]{:S(2)}, u32[]{:S(2)}) collective-permute-start(bf16[400,768]{1,0:T(8,128)(2,1)} %collective-permute-done.3.refs_0_), channel_id=1, source_target_pairs={{0,2},{2,0},{4,6},{6,4},{8,10},{10,8},{12,14},{14,12},{16,18},{18,... | collective-permute-start | bytes 1843208 | tf_op jit(solution)/shard_map/ppermute | solution.py:549
  59.7 15.3 %collective-permute-start.9 = (bf16[400,768]{1,0:T(8,128)(2,1)}, bf16[400,768]{1,0:T(8,128)(2,1)S(1)}, u32[]{:S(2)}, u32[]{:S(2)}) collective-permute-start(bf16[400,768]{1,0:T(8,128)(2,1)} %collective-permute-done.6.refs_1_), channel_id=1, source_target_pairs={{0,2},{2,0},{4,6},{6,4},{8,10},{10,8},{12,14},{14,12},{16,18},{18,... | collective-permute-start | bytes 1843208 | tf_op jit(solution)/shard_map/ppermute | solution.py:549
  138.6 25.8 %collective-permute-start.15 = (bf16[768,768]{1,0:T(8,128)(2,1)}, bf16[768,768]{1,0:T(8,128)(2,1)}, u32[]{:S(2)}, u32[]{:S(2)}) collective-permute-start(bf16[768,768]{1,0:T(8,128)(2,1)} %fusion.19), channel_id=1, source_target_pairs={{0,2},{2,0},{4,6},{6,4},{8,10},{10,8},{12,14},{14,12},{16,18},{18,... | collective-permute-start | bytes 3538952 | tf_op jit(solution)/shard_map/ppermute | solution.py:549
  138.7 29.1 %collective-permute-start.16 = (bf16[768,768]{1,0:T(8,128)(2,1)}, bf16[768,768]{1,0:T(8,128)(2,1)}, u32[]{:S(2)}, u32[]{:S(2)}) collective-permute-start(bf16[768,768]{1,0:T(8,128)(2,1)} %add_convert_fusion.7), channel_id=1, source_target_pairs={{0,1},{1,0},{2,3},{3,2},{4,5},{5,4},{6,7},{7,6},{8,9},{9,8},{10,11... | collective-permute-start | bytes 3538952 | tf_op jit(solution)/shard_map/ppermute | solution.py:544
  162.9 39.5 %collective-permute-start.20 = (bf16[768,768]{1,0:T(8,128)(2,1)}, bf16[768,768]{1,0:T(8,128)(2,1)}, u32[]{:S(2)}, u32[]{:S(2)}) collective-permute-start(bf16[768,768]{1,0:T(8,128)(2,1)} %add_convert_fusion.5), channel_id=1, source_target_pairs={{0,1},{1,0},{2,3},{3,2},{4,5},{5,4},{6,7},{7,6},{8,9},{9,8},{10,11... | collective-permute-start | bytes 3538952 | tf_op jit(solution)/shard_map/ppermute | solution.py:544
  170.4 27.1 %collective-permute-start.18 = (bf16[384,768]{1,0:T(8,128)(2,1)}, bf16[384,768]{1,0:T(8,128)(2,1)}, u32[]{:S(2)}, u32[]{:S(2)}) collective-permute-start(bf16[384,768]{1,0:T(8,128)(2,1)} %constant_dynamic-slice_fusion.9), channel_id=1, source_target_pairs={{0,8},{2,10},{4,12},{6,14},{8,0},{10,2},{12,4},{14,6},{16,24},{18,... | collective-permute-start | bytes 1769480 | tf_op jit(solution)/shard_map/ppermute | solution.py:549
  173.9 26.7 %collective-permute-start.19 = (bf16[384,768]{1,0:T(8,128)(2,1)}, bf16[384,768]{1,0:T(8,128)(2,1)}, u32[]{:S(2)}, u32[]{:S(2)}) collective-permute-start(bf16[384,768]{1,0:T(8,128)(2,1)} %constant_dynamic-slice_fusion.8), channel_id=1, source_target_pairs={{0,4},{2,6},{4,0},{6,2},{8,12},{10,14},{12,8},{14,10},{16,20},{18,... | collective-permute-start | bytes 1769480 | tf_op jit(solution)/shard_map/ppermute | solution.py:549
  192.0 13.2 %collective-permute-start.21 = (bf16[768,768]{1,0:T(8,128)(2,1)}, bf16[768,768]{1,0:T(8,128)(2,1)}, u32[]{:S(2)}, u32[]{:S(2)}) collective-permute-start(bf16[768,768]{1,0:T(8,128)(2,1)} %bitcast.68), channel_id=1, source_target_pairs={{0,2},{2,0},{4,6},{6,4},{8,10},{10,8},{12,14},{14,12},{16,18},{18,... | collective-permute-start | bytes 3538952 | tf_op jit(solution)/shard_map/ppermute | solution.py:549
  201.9 22.9 %collective-permute-start.28 = (bf16[384,768]{1,0:T(8,128)(2,1)S(1)}, bf16[384,768]{1,0:T(8,128)(2,1)S(1)}, u32[]{:S(2)}, u32[]{:S(2)}) collective-permute-start(bf16[384,768]{1,0:T(8,128)(2,1)S(1)} %add_convert_fusion.11), channel_id=1, source_target_pairs={{0,1},{1,0},{2,3},{3,2},{4,5},{5,4},{6,7},{7,6},{8,9},{9,8},{10,11... | collective-permute-start | bytes 1769480 | tf_op jit(solution)/shard_map/ppermute | solution.py:544
  204.1 18.5 %collective-permute-start.23 = (bf16[384,768]{1,0:T(8,128)(2,1)S(1)}, bf16[384,768]{1,0:T(8,128)(2,1)S(1)}, u32[]{:S(2)}, u32[]{:S(2)}) collective-permute-start(bf16[384,768]{1,0:T(8,128)(2,1)S(1)} %constant_dynamic-slice_fusion.6), channel_id=1, source_target_pairs={{0,8},{2,10},{4,12},{6,14},{8,0},{10,2},{12,4},{14,6},{16,24},{18,... | collective-permute-start | bytes 1769480 | tf_op jit(solution)/shard_map/ppermute | solution.py:549
  206.9 17.8 %collective-permute-start.26 = (f32[16,768]{1,0:T(8,128)S(1)}, f32[16,768]{1,0:T(8,128)S(1)}, u32[]{:S(2)}, u32[]{:S(2)}) collective-permute-start(f32[16,768]{1,0:T(8,128)S(1)} %copy-done.57), channel_id=1, source_target_pairs={{0,1},{1,0},{2,3},{3,2},{4,5},{5,4},{6,7},{7,6},{8,9},{9,8},{10,11... | collective-permute-start | bytes 147464 | tf_op jit(solution)/shard_map/ppermute | solution.py:544
  208.6 15.9 %collective-permute-start.24 = (bf16[384,768]{1,0:T(8,128)(2,1)S(1)}, bf16[384,768]{1,0:T(8,128)(2,1)S(1)}, u32[]{:S(2)}, u32[]{:S(2)}) collective-permute-start(bf16[384,768]{1,0:T(8,128)(2,1)S(1)} %constant_dynamic-slice_fusion.5), channel_id=1, source_target_pairs={{0,4},{2,6},{4,0},{6,2},{8,12},{10,14},{12,8},{14,10},{16,20},{18,... | collective-permute-start | bytes 1769480 | tf_op jit(solution)/shard_map/ppermute | solution.py:549
  209.2 15.4 %collective-permute-start.25 = (bf16[96,768]{1,0:T(8,128)(2,1)S(1)}, bf16[96,768]{1,0:T(8,128)(2,1)S(1)}, u32[]{:S(2)}, u32[]{:S(2)}) collective-permute-start(bf16[96,768]{1,0:T(8,128)(2,1)S(1)} %constant_dynamic-slice_fusion.4), channel_id=1, source_target_pairs={{0,16},{2,18},{4,20},{6,22},{8,24},{10,26},{12,28},{14,30},{16,0},... | collective-permute-start | bytes 442376 | tf_op jit(solution)/shard_map/ppermute | solution.py:549
  224.7 11.6 %collective-permute-start.30 = (f32[16,768]{1,0:T(8,128)S(1)}, f32[16,768]{1,0:T(8,128)S(1)}, u32[]{:S(2)}, u32[]{:S(2)}) collective-permute-start(f32[16,768]{1,0:T(8,128)S(1)} %add.181), channel_id=1, source_target_pairs={{0,2},{2,0},{4,6},{6,4},{8,10},{10,8},{12,14},{14,12},{16,18},{18,... | collective-permute-start | bytes 147464 | tf_op jit(solution)/shard_map/ppermute | solution.py:549
  224.9 10.9 %collective-permute-start.27 = (bf16[96,768]{1,0:T(8,128)(2,1)S(1)}, bf16[96,768]{1,0:T(8,128)(2,1)S(1)}, u32[]{:S(2)}, u32[]{:S(2)}) collective-permute-start(bf16[96,768]{1,0:T(8,128)(2,1)S(1)} %add_convert_fusion.18.refs_0_), channel_id=1, source_target_pairs={{0,16},{2,18},{4,20},{6,22},{8,24},{10,26},{12,28},{14,30},{16,0},... | collective-permute-start | bytes 442376 | tf_op jit(solution)/shard_map/ppermute | solution.py:549
  226.3 15.6 %collective-permute-start.32 = (bf16[192,768]{1,0:T(8,128)(2,1)S(1)}, bf16[192,768]{1,0:T(8,128)(2,1)S(1)}, u32[]{:S(2)}, u32[]{:S(2)}) collective-permute-start(bf16[192,768]{1,0:T(8,128)(2,1)S(1)} %constant_dynamic-slice_fusion.2), channel_id=1, source_target_pairs={{0,8},{2,10},{4,12},{6,14},{8,0},{10,2},{12,4},{14,6},{16,24},{18,... | collective-permute-start | bytes 884744 | tf_op jit(solution)/shard_map/ppermute | solution.py:549
  231.0 11.2 %collective-permute-start.33 = (bf16[96,768]{1,0:T(8,128)(2,1)S(1)}, bf16[96,768]{1,0:T(8,128)(2,1)S(1)}, u32[]{:S(2)}, u32[]{:S(2)}) collective-permute-start(bf16[96,768]{1,0:T(8,128)(2,1)S(1)} %constant_dynamic-slice_fusion.1), channel_id=1, source_target_pairs={{0,16},{2,18},{4,20},{6,22},{8,24},{10,26},{12,28},{14,30},{16,0},... | collective-permute-start | bytes 442376 | tf_op jit(solution)/shard_map/ppermute | solution.py:549
  244.1 23.7 %collective-permute-start.35 = (bf16[384,768]{1,0:T(8,128)(2,1)S(1)}, bf16[384,768]{1,0:T(8,128)(2,1)S(1)}, u32[]{:S(2)}, u32[]{:S(2)}) collective-permute-start(bf16[384,768]{1,0:T(8,128)(2,1)S(1)} %pad_maximum_fusion.3), channel_id=1, source_target_pairs={{0,8},{2,10},{4,12},{6,14},{8,0},{10,2},{12,4},{14,6},{16,24},{18,... | collective-permute-start | bytes 1769480 | tf_op jit(solution)/shard_map/ppermute | solution.py:549
  245.9 16.1 %collective-permute-start.36 = (bf16[96,768]{1,0:T(8,128)(2,1)S(1)}, bf16[96,768]{1,0:T(8,128)(2,1)S(1)}, u32[]{:S(2)}, u32[]{:S(2)}) collective-permute-start(bf16[96,768]{1,0:T(8,128)(2,1)S(1)} %add_convert_fusion.17.refs_0_), channel_id=1, source_target_pairs={{0,16},{2,18},{4,20},{6,22},{8,24},{10,26},{12,28},{14,30},{16,0},... | collective-permute-start | bytes 442376 | tf_op jit(solution)/shard_map/ppermute | solution.py:549
  251.3 14.7 %collective-permute-start.40 = (bf16[96,768]{1,0:T(8,128)(2,1)S(1)}, bf16[96,768]{1,0:T(8,128)(2,1)S(1)}, u32[]{:S(2)}, u32[]{:S(2)}) collective-permute-start(bf16[96,768]{1,0:T(8,128)(2,1)S(1)} %add_convert_fusion.16.refs_0_), channel_id=1, source_target_pairs={{0,16},{2,18},{4,20},{6,22},{8,24},{10,26},{12,28},{14,30},{16,0},... | collective-permute-start | bytes 442376 | tf_op jit(solution)/shard_map/ppermute | solution.py:549
  270.6 10.3 %collective-permute-start.42 = (bf16[192,768]{1,0:T(8,128)(2,1)S(1)}, bf16[192,768]{1,0:T(8,128)(2,1)S(1)}, u32[]{:S(2)}, u32[]{:S(2)}) collective-permute-start(bf16[192,768]{1,0:T(8,128)(2,1)S(1)} %pad_maximum_fusion.8), channel_id=1, source_target_pairs={{0,8},{2,10},{4,12},{6,14},{8,0},{10,2},{12,4},{14,6},{16,24},{18,... | collective-permute-start | bytes 884744 | tf_op jit(solution)/shard_map/ppermute | solution.py:549
  272.9 18.4 %collective-permute-start.44 = (bf16[384,768]{1,0:T(8,128)(2,1)S(1)}, bf16[384,768]{1,0:T(8,128)(2,1)S(1)}, u32[]{:S(2)}, u32[]{:S(2)}) collective-permute-start(bf16[384,768]{1,0:T(8,128)(2,1)S(1)} %pad_maximum_fusion.4), channel_id=1, source_target_pairs={{0,8},{2,10},{4,12},{6,14},{8,0},{10,2},{12,4},{14,6},{16,24},{18,... | collective-permute-start | bytes 1769480 | tf_op jit(solution)/shard_map/ppermute | solution.py:549
  280.9 11.7 %collective-permute-start.43 = (bf16[384,768]{1,0:T(8,128)(2,1)S(1)}, bf16[384,768]{1,0:T(8,128)(2,1)S(1)}, u32[]{:S(2)}, u32[]{:S(2)}) collective-permute-start(bf16[384,768]{1,0:T(8,128)(2,1)S(1)} %pad_maximum_fusion.5), channel_id=1, source_target_pairs={{0,4},{2,6},{4,0},{6,2},{8,12},{10,14},{12,8},{14,10},{16,20},{18,... | collective-permute-start | bytes 1769480 | tf_op jit(solution)/shard_map/ppermute | solution.py:549
  281.8 14.2 %collective-permute-start.47 = (bf16[768,768]{1,0:T(8,128)(2,1)}, bf16[768,768]{1,0:T(8,128)(2,1)}, u32[]{:S(2)}, u32[]{:S(2)}) collective-permute-start(bf16[768,768]{1,0:T(8,128)(2,1)} %pad_maximum_fusion), channel_id=1, source_target_pairs={{0,2},{2,0},{4,6},{6,4},{8,10},{10,8},{12,14},{14,12},{16,18},{18,... | collective-permute-start | bytes 3538952 | tf_op jit(solution)/shard_map/ppermute | solution.py:549
  (81 other events, 497.4 us)

commit v2 on v1

--- a/solution.py
+++ b/solution.py
@@ -833,7 +833,7 @@
     last = attn.hop("m", last)
     small_got = over_mp(tie(small_send, last))
     count, bit = lax.axis_size("dp"), 1
-    for what in "duadsaudsaudsaudsausgauap":
+    for what in "duadsaudsaudsaudasusgapua":
         if what == "s":
             last = small = tie(small, last) + small_got
             if bit < count:
@@ -847,6 +847,8 @@
             down.held[0] = tie(down.held[0], last)
             (grad_down,) = place(place_kernel, down.held, down.spots(me), w_down.shape)
             last = grad_down
+            up.held[-1] = tie(up.held[-1], last)
+            attn.held[-1] = tie(attn.held[-1], last)
         else:
             last = {"d": down, "u": up, "a": attn}[what].hop("m", last)
     if bit > 16:

time: 311 us -> 308 us (level)
    unnamed x130 -> x122, local copies, waits for them, and re-layouts: 10 us -> 10 us
  transfers between devices with their start and end apart: 48 -> 48, of which waited for: 17 -> 19; matrix products, arithmetic and copies ran while one was open for 14% -> 14% of each run, Pallas kernels for 29% -> 29%
where the time goes in v2:
time: 308 us; the launch traced here: 306 us
  Pallas kernels  136 us (44%)
  waiting for transfers between devices  60 us (19%)
  starting transfers between devices  44.1 us (14%)
  other arithmetic  21.1 us (7%)
  matrix products  19.5 us (6%)
  local copies, waits for them, and re-layouts  18.7 us (6%)
  between operations  7.35 us (2%)
    ppermute x41, waiting for transfers between devices, over_dp(): return lax.ppermute(x, 'dp', [(i, i ^ bit) for i in range(n)])  55.7 us
    pallas_call x1, Pallas kernels, ffn_back(): pl.pallas_call(ffn_back_kernel, grid_spec=pltpu.PrefetchScalarGridSpec(nu...  39 us
    ppermute x41, starting transfers between devices, over_dp(): return lax.ppermute(x, 'dp', [(i, i ^ bit) for i in range(n)])  35.4 us
    pallas_call x2, Pallas kernels, attn_bwd(): pl.pallas_call(attn_bwd_kernel, grid_spec=pltpu.PrefetchScalarGridSpec(nu...  33.9 us
    pallas_call x3, Pallas kernels, attn_fwd(): pl.pallas_call(kernel, grid_spec=pltpu.PrefetchScalarGridSpec(num_scalar_...  26.1 us
    convert_element_type x19, other arithmetic, land(): total = (x.astype(F32) + got.astype(F32)).astype(BF16)  17.4 us
    pallas_call x1, Pallas kernels, ffn_front(): pl.pallas_call(ffn_front_kernel, grid_spec=pltpu.PrefetchScalarGridSpec(n...  15 us
    dot_general x8, matrix products, dot(): return lax.dot_general(a, b, dims, preferred_element_type=F32)  13.9 us
  transfers between devices with their start and end apart: 48, of which 19 were waited for; matrix products, arithmetic and copies ran while one was open for 14% of the time, Pallas kernels for 29%

profile of v2, /device:TPU:0, one launch (start us, length us, event | category | flops | bytes accessed | tf_op | source)
XLA Modules:
  0.0 306.5 jit_solution(8657373019569719857)
XLA Ops:
  1.8 2.6 pack_attn.1
  4.4 2.9 collective-permute-start
  8.0 3.5 %pack_ffn.1 = (bf16[400,768]{1,0:T(8,128)(2,1)}, bf16[384,768]{1,0:T(8,128)(2,1)}, bf16[2,512,128]{2,1,0:T(8,128)(2,1)}, bf16[2,512,128]{2,1,0:T(8,128)(2,1)}) custom-call(s32[13]{0:T(128)} %or_select_fusion.info_ref.refs_0_.at_ref, s32[4,4]{1,0:T(4,128)} %seg_ref.1, bf16[768,1536]{1,0:T(8,128)(2,1)} %wu_m_ref.1, bf16[1536,768]{1,0:T(8,128)(2,1)} %wd_m_ref.1, ...), custom_call_target="tpu_custom_call" | custom-call | bytes 33554432 | tf_op jit(solution)/shard_map/pack_ffn/pallas_call | solution.py:484
  13.5 8.7 %attn_fwd.3 = (bf16[3,1024,384]{2,1,0:T(8,128)(2,1)}, bf16[1024,384]{1,0:T(8,128)(2,1)S(1)}, bf16[12,512,512]{2,1,0:T(8,128)(2,1)}, f32[2,3,2,512]{3,2,1,0:T(2,128)S(1)}) custom-call(s32[13]{0:T(128)S(1)} %copy-done.19, s32[4]{0:T(128)S(1)} %copy-done.27, bf16[1024,768]{1,0:T(8,128)(2,1)S(1)} %copy-done.1, bf16[3,768,384]{2,1,0:T(8,128)(2,1)S(1)} %copy-done, ...), custom_call_target="tpu_custom_call" | custom-call | flops 800000 | bytes 8000 | tf_op jit(solution)/shard_map/attn_fwd/pallas_call | solution.py:86
  24.5 5.1 %attn_fwd.4 = (bf16[3,1024,384]{2,1,0:T(8,128)(2,1)}, bf16[1024,384]{1,0:T(8,128)(2,1)S(1)}, bf16[12,512,512]{2,1,0:T(8,128)(2,1)}, f32[2,3,2,512]{3,2,1,0:T(2,128)S(1)}) custom-call(s32[13]{0:T(128)S(1)} %copy-done.19, s32[4]{0:T(128)S(1)} %copy-done.27, ...), custom_call_target="tpu_custom_call", output_to_operand_aliasing={{0}: (7, {}), {1}: (8, {}), {2}: (9, {}), {3}: (10, {})} | custom-call | flops 800000 | bytes 8000 | tf_op jit(solution)/shard_map/attn_fwd/pallas_call | solution.py:86
  31.1 3.6 %collective-permute-done.3.refs_0_ = bf16[400,768]{1,0:T(8,128)(2,1)} collective-permute-done((bf16[400,768]{1,0:T(8,128)(2,1)}, bf16[400,768]{1,0:T(8,128)(2,1)}, u32[]{:S(2)}, u32[]{:S(2)}) %collective-permute-start.3) | collective-permute-done | bytes 614432 | tf_op jit(solution)/shard_map/ppermute | solution.py:544
  35.5 3.8 %collective-permute-done.1.refs_1_ = bf16[400,768]{1,0:T(8,128)(2,1)} collective-permute-done((bf16[400,768]{1,0:T(8,128)(2,1)}, bf16[400,768]{1,0:T(8,128)(2,1)}, u32[]{:S(2)}, u32[]{:S(2)}) %collective-permute-start.1) | collective-permute-done | bytes 614432 | tf_op jit(solution)/shard_map/ppermute | solution.py:549
  45.6 12.3 %attn_fwd.5 = (bf16[3,1024,384]{2,1,0:T(8,128)(2,1)}, bf16[1024,384]{1,0:T(8,128)(2,1)S(1)}, bf16[12,512,512]{2,1,0:T(8,128)(2,1)}, f32[2,3,2,512]{3,2,1,0:T(2,128)S(1)}) custom-call(s32[13]{0:T(128)S(1)} %copy-done.19, s32[4]{0:T(128)S(1)} %copy-done.27, bf16[1024,768]{1,0:T(8,128)(2,1)S(1)} %copy-done.1, ...), custom_call_target="tpu_custom_call" | custom-call | flops 800000 | bytes 8000 | tf_op jit(solution)/shard_map/attn_fwd/pallas_call | solution.py:86
  60.1 15.0 %ffn_front.1 = (bf16[1024,768]{1,0:T(8,128)(2,1)S(1)}, f32[1024,768]{1,0:T(8,128)}, f32[1024,1]{1,0:T(8,128)S(1)}, f32[1024,768]{1,0:T(8,128)}, bf16[2,1024,768]...) custom-call(s32[13]{0:T(128)S(1)} %copy-done.19, bf16[1024,384]{1,0:T(8,128)(2,1)S(1)} %copy-done.13, ...), custom_call_target="tpu_custom_call" | custom-call | flops 80000000000 | bytes 150994944 | tf_op jit(solution)/shard_map/ffn_front/pallas_call | solution.py:304
  80.4 39.0 %ffn_back.1 = (bf16[1024,768]{1,0:T(8,128)(2,1)}, f32[2,768]{1,0:T(2,128)}, bf16[2,1024,768]{2,1,0:T(8,128)(2,1)}, bf16[1024,768]{1,0:T(8,128)(2,1)S(1)}, bf16[2...) custom-call(s32[13]{0:T(128)S(1)} %copy-done.19, ...), custom_call_target="tpu_custom_call" | custom-call | flops 199999995904 | bytes 251658240 | tf_op jit(solution)/shard_map/ffn_back/pallas_call | solution.py:391
  119.4 2.6 slice_bitcast_fusion.2
  136.3 2.5 fusion.19
  140.9 2.7 fusion.22
  143.7 16.8 %attn_bwd.2 = (bf16[3,1024,384]{2,1,0:T(8,128)(2,1)}, bf16[2,384,768]{2,1,0:T(8,128)(2,1)}, bf16[2,384,768]{2,1,0:T(8,128)(2,1)}, f32[2,384]{1,0:T(2,128)S(1)}) custom-call(s32[13]{0:T(128)S(1)} %copy-done.19, bf16[1024,768]{1,0:T(8,128)(2,1)S(1)} %copy-done.2, bf16[1024,768]{1,0:T(8,128)(2,1)S(1)} %get-tuple-element.194.ga_ref, ...), custom_call_target="tpu_custom_call" | custom-call | flops 128000000000 | bytes 50331648 | tf_op jit(solution)/shard_map/attn_bwd/pallas_call | solution.py:191
  164.5 3.1 add_convert_fusion.4
  174.5 17.1 %attn_bwd.3 = (bf16[3,1024,384]{2,1,0:T(8,128)(2,1)}, bf16[2,384,768]{2,1,0:T(8,128)(2,1)}, bf16[2,384,768]{2,1,0:T(8,128)(2,1)}, f32[2,384]{1,0:T(2,128)S(1)}) custom-call(s32[13]{0:T(128)S(1)} %copy-done.19, bf16[1024,768]{1,0:T(8,128)(2,1)S(1)} %copy-done.2, bf16[1024,768]{1,0:T(8,128)(2,1)S(1)} %copy-done.36, bf16[384,768]{1,0:T(8,128)(2,1)S(1)} %copy-done.18, ...), custom_call_target="tpu_custom_call" | custom-call | flops 128000000000 | bytes 50331648 | tf_op jit(solution)/shard_map/attn_bwd/pallas_call | solution.py:191
  209.3 2.7 collective-permute-start.25
  212.0 10.7 %collective-permute-done.23 = bf16[384,768]{1,0:T(8,128)(2,1)S(1)} collective-permute-done((bf16[384,768]{1,0:T(8,128)(2,1)S(1)}, bf16[384,768]{1,0:T(8,128)(2,1)S(1)}, u32[]{:S(2)}, u32[]{:S(2)}) %collective-permute-start.23) | collective-permute-done | bytes 589856 | tf_op jit(solution)/shard_map/ppermute | solution.py:549
  226.5 2.4 collective-permute-start.32
  232.4 3.5 %collective-permute-done.27.refs_1_ = bf16[96,768]{1,0:T(8,128)(2,1)S(1)} collective-permute-done((bf16[96,768]{1,0:T(8,128)(2,1)S(1)}, bf16[96,768]{1,0:T(8,128)(2,1)S(1)}, u32[]{:S(2)}, u32[]{:S(2)}) %collective-permute-start.27) | collective-permute-done | bytes 147488 | tf_op jit(solution)/shard_map/ppermute | solution.py:549
  236.4 5.6 %collective-permute-done.32 = bf16[192,768]{1,0:T(8,128)(2,1)S(1)} collective-permute-done((bf16[192,768]{1,0:T(8,128)(2,1)S(1)}, bf16[192,768]{1,0:T(8,128)(2,1)S(1)}, u32[]{:S(2)}, u32[]{:S(2)}) %collective-permute-start.32) | collective-permute-done | bytes 294944 | tf_op jit(solution)/shard_map/ppermute | solution.py:549
  249.1 2.2 collective-permute-done.35
  251.7 10.5 %collective-permute-done.38.refs_1_ = bf16[96,768]{1,0:T(8,128)(2,1)S(1)} collective-permute-done((bf16[96,768]{1,0:T(8,128)(2,1)S(1)}, bf16[96,768]{1,0:T(8,128)(2,1)S(1)}, u32[]{:S(2)}, u32[]{:S(2)}) %collective-permute-start.38) | collective-permute-done | bytes 147488 | tf_op jit(solution)/shard_map/ppermute | solution.py:549
  263.1 3.0 collective-permute-start.39
  268.5 2.2 collective-permute-start.41
  273.7 2.2 fusion.37
  276.3 3.4 %fusion = bf16[1024,768]{1,0:T(8,128)(2,1)} fusion(f32[1024,768]{1,0:T(8,128)S(1)} %copy-done.56, f32[1024,768,1]{1,0,2:T(8,128)S(1)} %fusion.37, bf16[3,1024,384]{2,1,0:T(8,128)(2,1)S(1)} %copy-done.57, bf16[3,768,384]{2,1,0:T(8,128)(2,1)S(1)} %copy-done), kind=kOutput, calls=%fused_computation.1 | convolution fusion | flops 1814298624 | bytes 11993088 | tf_op jit(solution)/shard_map/cte,cde->td/dot_general | solution.py:803
  282.0 3.0 place_kernel.1
  285.0 6.3 %collective-permute-done.45.refs_3_ = bf16[384,768]{1,0:T(8,128)(2,1)S(1)} collective-permute-done((bf16[384,768]{1,0:T(8,128)(2,1)S(1)}, bf16[384,768]{1,0:T(8,128)(2,1)S(1)}, u32[]{:S(2)}, u32[]{:S(2)}) %collective-permute-start.45) | collective-permute-done | bytes 589856 | tf_op jit(solution)/shard_map/ppermute | solution.py:549
  292.5 2.1 collective-permute-done.43.refs_3_
  298.2 3.0 place_up_kernel.1
  301.3 4.7 %place_attn_kernel.1 = (f32[3,768,384]{2,1,0:T(8,128)}, f32[384,768]{1,0:T(8,128)}) custom-call(s32[16]{0:T(128)S(1)} %fusion.35.at_ref, bf16[96,768]{1,0:T(8,128)(2,1)S(1)} %add_convert_fusion.16.refs_0_, bf16[96,768]{1,0:T(8,128)(2,1)S(1)} %collective-permute-done.36.refs_1_, bf16[192,768]{1,0:T(8,128)(2,1)S(1)} %collective-permute-done.42.refs_2_, ...), custom_call_target="tpu_custom_call" | custom-call | bytes 56623104 | tf_op jit(solution)/shard_map/place_attn_kernel/pallas_call | solution.py:600
  (272 shorter events, 90.2 us)
Async XLA Ops:
  4.4 17.9 %collective-permute-start = (bf16[400,768]{1,0:T(8,128)(2,1)}, bf16[400,768]{1,0:T(8,128)(2,1)}, u32[]{:S(2)}, u32[]{:S(2)}) collective-permute-start(bf16[400,768]{1,0:T(8,128)(2,1)} %pack_attn.1), channel_id=1, source_target_pairs={{0,1},{1,0},{2,3},{3,2},{4,5},{5,4},{6,7},{7,6},{8,9},{9,8},{10,11... | collective-permute-start | bytes 1843208 | tf_op jit(solution)/shard_map/ppermute | solution.py:544
  11.5 23.2 %collective-permute-start.3 = (bf16[400,768]{1,0:T(8,128)(2,1)}, bf16[400,768]{1,0:T(8,128)(2,1)}, u32[]{:S(2)}, u32[]{:S(2)}) collective-permute-start(bf16[400,768]{1,0:T(8,128)(2,1)} %get-tuple-element.138), channel_id=1, source_target_pairs={{0,1},{1,0},{2,3},{3,2},{4,5},{5,4},{6,7},{7,6},{8,9},{9,8},{10,11... | collective-permute-start | bytes 1843208 | tf_op jit(solution)/shard_map/ppermute | solution.py:544
  22.4 12.3 %collective-permute-start.2 = (bf16[400,768]{1,0:T(8,128)(2,1)}, bf16[400,768]{1,0:T(8,128)(2,1)S(1)}, u32[]{:S(2)}, u32[]{:S(2)}) collective-permute-start(bf16[400,768]{1,0:T(8,128)(2,1)} %collective-permute-done.refs_0_), channel_id=1, source_target_pairs={{0,2},{2,0},{4,6},{6,4},{8,10},{10,8},{12,14},{14,12},{16,18},{18,... | collective-permute-start | bytes 1843208 | tf_op jit(solution)/shard_map/ppermute | solution.py:549
  22.4 16.9 %collective-permute-start.1 = (bf16[400,768]{1,0:T(8,128)(2,1)}, bf16[400,768]{1,0:T(8,128)(2,1)}, u32[]{:S(2)}, u32[]{:S(2)}) collective-permute-start(bf16[400,768]{1,0:T(8,128)(2,1)} %collective-permute-done.refs_0_), channel_id=1, source_target_pairs={{0,4},{2,6},{4,0},{6,2},{8,12},{10,14},{12,8},{14,10},{16,20},{18,... | collective-permute-start | bytes 1843208 | tf_op jit(solution)/shard_map/ppermute | solution.py:549
  39.3 18.5 %collective-permute-start.6 = (bf16[400,768]{1,0:T(8,128)(2,1)}, bf16[400,768]{1,0:T(8,128)(2,1)}, u32[]{:S(2)}, u32[]{:S(2)}) collective-permute-start(bf16[400,768]{1,0:T(8,128)(2,1)} %collective-permute-done.3.refs_0_), channel_id=1, source_target_pairs={{0,4},{2,6},{4,0},{6,2},{8,12},{10,14},{12,8},{14,10},{16,20},{18,... | collective-permute-start | bytes 1843208 | tf_op jit(solution)/shard_map/ppermute | solution.py:549
  41.0 16.8 %collective-permute-start.5 = (bf16[384,768]{1,0:T(8,128)(2,1)}, bf16[384,768]{1,0:T(8,128)(2,1)}, u32[]{:S(2)}, u32[]{:S(2)}) collective-permute-start(bf16[384,768]{1,0:T(8,128)(2,1)} %get-tuple-element.145), channel_id=1, source_target_pairs={{0,1},{1,0},{2,3},{3,2},{4,5},{5,4},{6,7},{7,6},{8,9},{9,8},{10,11... | collective-permute-start | bytes 1769480 | tf_op jit(solution)/shard_map/ppermute | solution.py:544
  57.9 17.2 %collective-permute-start.10 = (bf16[384,768]{1,0:T(8,128)(2,1)}, bf16[384,768]{1,0:T(8,128)(2,1)S(1)}, u32[]{:S(2)}, u32[]{:S(2)}) collective-permute-start(bf16[384,768]{1,0:T(8,128)(2,1)} %collective-permute-done.5.refs_4_), channel_id=1, source_target_pairs={{0,2},{2,0},{4,6},{6,4},{8,10},{10,8},{12,14},{14,12},{16,18},{18,... | collective-permute-start | bytes 1769480 | tf_op jit(solution)/shard_map/ppermute | solution.py:549
  57.9 17.1 %collective-permute-start.7 = (bf16[384,768]{1,0:T(8,128)(2,1)}, bf16[384,768]{1,0:T(8,128)(2,1)S(1)}, u32[]{:S(2)}, u32[]{:S(2)}) collective-permute-start(bf16[384,768]{1,0:T(8,128)(2,1)} %collective-permute-done.5.refs_4_), channel_id=1, source_target_pairs={{0,8},{2,10},{4,12},{6,14},{8,0},{10,2},{12,4},{14,6},{16,24},{18,... | collective-permute-start | bytes 1769480 | tf_op jit(solution)/shard_map/ppermute | solution.py:549
  59.6 15.5 %collective-permute-start.8 = (bf16[400,768]{1,0:T(8,128)(2,1)}, bf16[400,768]{1,0:T(8,128)(2,1)S(1)}, u32[]{:S(2)}, u32[]{:S(2)}) collective-permute-start(bf16[400,768]{1,0:T(8,128)(2,1)} %collective-permute-done.3.refs_0_), channel_id=1, source_target_pairs={{0,2},{2,0},{4,6},{6,4},{8,10},{10,8},{12,14},{14,12},{16,18},{18,... | collective-permute-start | bytes 1843208 | tf_op jit(solution)/shard_map/ppermute | solution.py:549
  59.7 15.4 %collective-permute-start.9 = (bf16[400,768]{1,0:T(8,128)(2,1)}, bf16[400,768]{1,0:T(8,128)(2,1)S(1)}, u32[]{:S(2)}, u32[]{:S(2)}) collective-permute-start(bf16[400,768]{1,0:T(8,128)(2,1)} %collective-permute-done.6.refs_1_), channel_id=1, source_target_pairs={{0,2},{2,0},{4,6},{6,4},{8,10},{10,8},{12,14},{14,12},{16,18},{18,... | collective-permute-start | bytes 1843208 | tf_op jit(solution)/shard_map/ppermute | solution.py:549
  138.7 25.7 %collective-permute-start.15 = (bf16[768,768]{1,0:T(8,128)(2,1)}, bf16[768,768]{1,0:T(8,128)(2,1)}, u32[]{:S(2)}, u32[]{:S(2)}) collective-permute-start(bf16[768,768]{1,0:T(8,128)(2,1)} %fusion.19), channel_id=1, source_target_pairs={{0,2},{2,0},{4,6},{6,4},{8,10},{10,8},{12,14},{14,12},{16,18},{18,... | collective-permute-start | bytes 3538952 | tf_op jit(solution)/shard_map/ppermute | solution.py:549
  138.9 29.1 %collective-permute-start.16 = (bf16[768,768]{1,0:T(8,128)(2,1)}, bf16[768,768]{1,0:T(8,128)(2,1)}, u32[]{:S(2)}, u32[]{:S(2)}) collective-permute-start(bf16[768,768]{1,0:T(8,128)(2,1)} %add_convert_fusion.7), channel_id=1, source_target_pairs={{0,1},{1,0},{2,3},{3,2},{4,5},{5,4},{6,7},{7,6},{8,9},{9,8},{10,11... | collective-permute-start | bytes 3538952 | tf_op jit(solution)/shard_map/ppermute | solution.py:544
  163.0 39.5 %collective-permute-start.20 = (bf16[768,768]{1,0:T(8,128)(2,1)}, bf16[768,768]{1,0:T(8,128)(2,1)}, u32[]{:S(2)}, u32[]{:S(2)}) collective-permute-start(bf16[768,768]{1,0:T(8,128)(2,1)} %add_convert_fusion.5), channel_id=1, source_target_pairs={{0,1},{1,0},{2,3},{3,2},{4,5},{5,4},{6,7},{7,6},{8,9},{9,8},{10,11... | collective-permute-start | bytes 3538952 | tf_op jit(solution)/shard_map/ppermute | solution.py:544
  170.5 27.1 %collective-permute-start.18 = (bf16[384,768]{1,0:T(8,128)(2,1)}, bf16[384,768]{1,0:T(8,128)(2,1)}, u32[]{:S(2)}, u32[]{:S(2)}) collective-permute-start(bf16[384,768]{1,0:T(8,128)(2,1)} %constant_dynamic-slice_fusion.9), channel_id=1, source_target_pairs={{0,8},{2,10},{4,12},{6,14},{8,0},{10,2},{12,4},{14,6},{16,24},{18,... | collective-permute-start | bytes 1769480 | tf_op jit(solution)/shard_map/ppermute | solution.py:549
  174.1 26.7 %collective-permute-start.19 = (bf16[384,768]{1,0:T(8,128)(2,1)}, bf16[384,768]{1,0:T(8,128)(2,1)}, u32[]{:S(2)}, u32[]{:S(2)}) collective-permute-start(bf16[384,768]{1,0:T(8,128)(2,1)} %constant_dynamic-slice_fusion.8), channel_id=1, source_target_pairs={{0,4},{2,6},{4,0},{6,2},{8,12},{10,14},{12,8},{14,10},{16,20},{18,... | collective-permute-start | bytes 1769480 | tf_op jit(solution)/shard_map/ppermute | solution.py:549
  192.1 13.2 %collective-permute-start.21 = (bf16[768,768]{1,0:T(8,128)(2,1)}, bf16[768,768]{1,0:T(8,128)(2,1)}, u32[]{:S(2)}, u32[]{:S(2)}) collective-permute-start(bf16[768,768]{1,0:T(8,128)(2,1)} %bitcast.68), channel_id=1, source_target_pairs={{0,2},{2,0},{4,6},{6,4},{8,10},{10,8},{12,14},{14,12},{16,18},{18,... | collective-permute-start | bytes 3538952 | tf_op jit(solution)/shard_map/ppermute | solution.py:549
  199.0 10.2 %collective-permute-start.22 = (bf16[192,768]{1,0:T(8,128)(2,1)S(1)}, bf16[192,768]{1,0:T(8,128)(2,1)S(1)}, u32[]{:S(2)}, u32[]{:S(2)}) collective-permute-start(bf16[192,768]{1,0:T(8,128)(2,1)S(1)} %constant_dynamic-slice_fusion.7), channel_id=1, source_target_pairs={{0,4},{2,6},{4,0},{6,2},{8,12},{10,14},{12,8},{14,10},{16,20},{18,... | collective-permute-start | bytes 884744 | tf_op jit(solution)/shard_map/ppermute | solution.py:549
  202.0 22.9 %collective-permute-start.28 = (bf16[384,768]{1,0:T(8,128)(2,1)S(1)}, bf16[384,768]{1,0:T(8,128)(2,1)S(1)}, u32[]{:S(2)}, u32[]{:S(2)}) collective-permute-start(bf16[384,768]{1,0:T(8,128)(2,1)S(1)} %add_convert_fusion.11), channel_id=1, source_target_pairs={{0,1},{1,0},{2,3},{3,2},{4,5},{5,4},{6,7},{7,6},{8,9},{9,8},{10,11... | collective-permute-start | bytes 1769480 | tf_op jit(solution)/shard_map/ppermute | solution.py:544
  204.2 18.5 %collective-permute-start.23 = (bf16[384,768]{1,0:T(8,128)(2,1)S(1)}, bf16[384,768]{1,0:T(8,128)(2,1)S(1)}, u32[]{:S(2)}, u32[]{:S(2)}) collective-permute-start(bf16[384,768]{1,0:T(8,128)(2,1)S(1)} %constant_dynamic-slice_fusion.6), channel_id=1, source_target_pairs={{0,8},{2,10},{4,12},{6,14},{8,0},{10,2},{12,4},{14,6},{16,24},{18,... | collective-permute-start | bytes 1769480 | tf_op jit(solution)/shard_map/ppermute | solution.py:549
  207.0 17.8 %collective-permute-start.26 = (f32[16,768]{1,0:T(8,128)S(1)}, f32[16,768]{1,0:T(8,128)S(1)}, u32[]{:S(2)}, u32[]{:S(2)}) collective-permute-start(f32[16,768]{1,0:T(8,128)S(1)} %copy-done.53), channel_id=1, source_target_pairs={{0,1},{1,0},{2,3},{3,2},{4,5},{5,4},{6,7},{7,6},{8,9},{9,8},{10,11... | collective-permute-start | bytes 147464 | tf_op jit(solution)/shard_map/ppermute | solution.py:544
  208.7 15.9 %collective-permute-start.24 = (bf16[384,768]{1,0:T(8,128)(2,1)S(1)}, bf16[384,768]{1,0:T(8,128)(2,1)S(1)}, u32[]{:S(2)}, u32[]{:S(2)}) collective-permute-start(bf16[384,768]{1,0:T(8,128)(2,1)S(1)} %constant_dynamic-slice_fusion.5), channel_id=1, source_target_pairs={{0,4},{2,6},{4,0},{6,2},{8,12},{10,14},{12,8},{14,10},{16,20},{18,... | collective-permute-start | bytes 1769480 | tf_op jit(solution)/shard_map/ppermute | solution.py:549
  209.3 15.4 %collective-permute-start.25 = (bf16[96,768]{1,0:T(8,128)(2,1)S(1)}, bf16[96,768]{1,0:T(8,128)(2,1)S(1)}, u32[]{:S(2)}, u32[]{:S(2)}) collective-permute-start(bf16[96,768]{1,0:T(8,128)(2,1)S(1)} %constant_dynamic-slice_fusion.4), channel_id=1, source_target_pairs={{0,16},{2,18},{4,20},{6,22},{8,24},{10,26},{12,28},{14,30},{16,0},... | collective-permute-start | bytes 442376 | tf_op jit(solution)/shard_map/ppermute | solution.py:549
  224.8 11.6 %collective-permute-start.30 = (f32[16,768]{1,0:T(8,128)S(1)}, f32[16,768]{1,0:T(8,128)S(1)}, u32[]{:S(2)}, u32[]{:S(2)}) collective-permute-start(f32[16,768]{1,0:T(8,128)S(1)} %add.181), channel_id=1, source_target_pairs={{0,2},{2,0},{4,6},{6,4},{8,10},{10,8},{12,14},{14,12},{16,18},{18,... | collective-permute-start | bytes 147464 | tf_op jit(solution)/shard_map/ppermute | solution.py:549
  225.1 10.9 %collective-permute-start.27 = (bf16[96,768]{1,0:T(8,128)(2,1)S(1)}, bf16[96,768]{1,0:T(8,128)(2,1)S(1)}, u32[]{:S(2)}, u32[]{:S(2)}) collective-permute-start(bf16[96,768]{1,0:T(8,128)(2,1)S(1)} %add_convert_fusion.18.refs_0_), channel_id=1, source_target_pairs={{0,16},{2,18},{4,20},{6,22},{8,24},{10,26},{12,28},{14,30},{16,0},... | collective-permute-start | bytes 442376 | tf_op jit(solution)/shard_map/ppermute | solution.py:549
  226.5 15.5 %collective-permute-start.32 = (bf16[192,768]{1,0:T(8,128)(2,1)S(1)}, bf16[192,768]{1,0:T(8,128)(2,1)S(1)}, u32[]{:S(2)}, u32[]{:S(2)}) collective-permute-start(bf16[192,768]{1,0:T(8,128)(2,1)S(1)} %constant_dynamic-slice_fusion.2), channel_id=1, source_target_pairs={{0,8},{2,10},{4,12},{6,14},{8,0},{10,2},{12,4},{14,6},{16,24},{18,... | collective-permute-start | bytes 884744 | tf_op jit(solution)/shard_map/ppermute | solution.py:549
  231.1 11.2 %collective-permute-start.33 = (bf16[96,768]{1,0:T(8,128)(2,1)S(1)}, bf16[96,768]{1,0:T(8,128)(2,1)S(1)}, u32[]{:S(2)}, u32[]{:S(2)}) collective-permute-start(bf16[96,768]{1,0:T(8,128)(2,1)S(1)} %constant_dynamic-slice_fusion.1), channel_id=1, source_target_pairs={{0,16},{2,18},{4,20},{6,22},{8,24},{10,26},{12,28},{14,30},{16,0},... | collective-permute-start | bytes 442376 | tf_op jit(solution)/shard_map/ppermute | solution.py:549
  244.2 23.7 %collective-permute-start.37 = (bf16[384,768]{1,0:T(8,128)(2,1)S(1)}, bf16[384,768]{1,0:T(8,128)(2,1)S(1)}, u32[]{:S(2)}, u32[]{:S(2)}) collective-permute-start(bf16[384,768]{1,0:T(8,128)(2,1)S(1)} %pad_maximum_fusion.3), channel_id=1, source_target_pairs={{0,8},{2,10},{4,12},{6,14},{8,0},{10,2},{12,4},{14,6},{16,24},{18,... | collective-permute-start | bytes 1769480 | tf_op jit(solution)/shard_map/ppermute | solution.py:549
  246.1 16.1 %collective-permute-start.38 = (bf16[96,768]{1,0:T(8,128)(2,1)S(1)}, bf16[96,768]{1,0:T(8,128)(2,1)S(1)}, u32[]{:S(2)}, u32[]{:S(2)}) collective-permute-start(bf16[96,768]{1,0:T(8,128)(2,1)S(1)} %add_convert_fusion.17.refs_0_), channel_id=1, source_target_pairs={{0,16},{2,18},{4,20},{6,22},{8,24},{10,26},{12,28},{14,30},{16,0},... | collective-permute-start | bytes 442376 | tf_op jit(solution)/shard_map/ppermute | solution.py:549
  251.4 14.7 %collective-permute-start.36 = (bf16[96,768]{1,0:T(8,128)(2,1)S(1)}, bf16[96,768]{1,0:T(8,128)(2,1)S(1)}, u32[]{:S(2)}, u32[]{:S(2)}) collective-permute-start(bf16[96,768]{1,0:T(8,128)(2,1)S(1)} %add_convert_fusion.16.refs_0_), channel_id=1, source_target_pairs={{0,16},{2,18},{4,20},{6,22},{8,24},{10,26},{12,28},{14,30},{16,0},... | collective-permute-start | bytes 442376 | tf_op jit(solution)/shard_map/ppermute | solution.py:549
  270.7 10.0 %collective-permute-start.42 = (bf16[192,768]{1,0:T(8,128)(2,1)S(1)}, bf16[192,768]{1,0:T(8,128)(2,1)S(1)}, u32[]{:S(2)}, u32[]{:S(2)}) collective-permute-start(bf16[192,768]{1,0:T(8,128)(2,1)S(1)} %pad_maximum_fusion.7), channel_id=1, source_target_pairs={{0,8},{2,10},{4,12},{6,14},{8,0},{10,2},{12,4},{14,6},{16,24},{18,... | collective-permute-start | bytes 884744 | tf_op jit(solution)/shard_map/ppermute | solution.py:549
  272.6 18.7 %collective-permute-start.45 = (bf16[384,768]{1,0:T(8,128)(2,1)S(1)}, bf16[384,768]{1,0:T(8,128)(2,1)S(1)}, u32[]{:S(2)}, u32[]{:S(2)}) collective-permute-start(bf16[384,768]{1,0:T(8,128)(2,1)S(1)} %pad_maximum_fusion.4), channel_id=1, source_target_pairs={{0,8},{2,10},{4,12},{6,14},{8,0},{10,2},{12,4},{14,6},{16,24},{18,... | collective-permute-start | bytes 1769480 | tf_op jit(solution)/shard_map/ppermute | solution.py:549
  280.7 13.8 %collective-permute-start.43 = (bf16[384,768]{1,0:T(8,128)(2,1)S(1)}, bf16[384,768]{1,0:T(8,128)(2,1)S(1)}, u32[]{:S(2)}, u32[]{:S(2)}) collective-permute-start(bf16[384,768]{1,0:T(8,128)(2,1)S(1)} %pad_maximum_fusion.5), channel_id=1, source_target_pairs={{0,4},{2,6},{4,0},{6,2},{8,12},{10,14},{12,8},{14,10},{16,20},{18,... | collective-permute-start | bytes 1769480 | tf_op jit(solution)/shard_map/ppermute | solution.py:549
  (77 other events, 483.1 us)

commit v3 on v2

--- a/solution.py
+++ b/solution.py
@@ -833,7 +833,7 @@
     last = attn.hop("m", last)
     small_got = over_mp(tie(small_send, last))
     count, bit = lax.axis_size("dp"), 1
-    for what in "duadsaudsaudsaudasusgapua":
+    for what in "dsuadaudsaudasudasusgapua":
         if what == "s":
             last = small = tie(small, last) + small_got
             if bit < count:

time: 308 us -> 306 us (level)
  waiting for transfers between devices: 60 us -> 56.8 us
    ppermute x41, waiting for transfers between devices: 55.7 us -> 45.9 us  [over_dp(): return lax.ppermute(x, 'dp', [(i, i ^ bit) for i in range(n)])]
    ppermute x7, waiting for transfers between devices: 4.32 us -> 10.8 us  [over_mp(): return lax.ppermute(x, 'mp', [(i, i ^ 1) for i in range(n)])]
where the time goes in v3:
time: 306 us; the launch traced here: 304 us
  Pallas kernels  136 us (44%)
  waiting for transfers between devices  56.8 us (19%)
  starting transfers between devices  45.1 us (15%)
  other arithmetic  21.1 us (7%)
  matrix products  19.5 us (6%)
  local copies, waits for them, and re-layouts  18.7 us (6%)
  between operations  7.39 us (2%)
    ppermute x41, waiting for transfers between devices, over_dp(): return lax.ppermute(x, 'dp', [(i, i ^ bit) for i in range(n)])  45.9 us
    pallas_call x1, Pallas kernels, ffn_back(): pl.pallas_call(ffn_back_kernel, grid_spec=pltpu.PrefetchScalarGridSpec(nu...  39 us
    ppermute x41, starting transfers between devices, over_dp(): return lax.ppermute(x, 'dp', [(i, i ^ bit) for i in range(n)])  36.4 us
    pallas_call x2, Pallas kernels, attn_bwd(): pl.pallas_call(attn_bwd_kernel, grid_spec=pltpu.PrefetchScalarGridSpec(nu...  33.9 us
    pallas_call x3, Pallas kernels, attn_fwd(): pl.pallas_call(kernel, grid_spec=pltpu.PrefetchScalarGridSpec(num_scalar_...  26.1 us
    convert_element_type x19, other arithmetic, land(): total = (x.astype(F32) + got.astype(F32)).astype(BF16)  17.4 us
    pallas_call x1, Pallas kernels, ffn_front(): pl.pallas_call(ffn_front_kernel, grid_spec=pltpu.PrefetchScalarGridSpec(n...  15 us
    dot_general x8, matrix products, dot(): return lax.dot_general(a, b, dims, preferred_element_type=F32)  13.9 us
  transfers between devices with their start and end apart: 48, of which 19 were waited for; matrix products, arithmetic and copies ran while one was open for 14% of the time, Pallas kernels for 29%

profile of v3, /device:TPU:0, one launch (start us, length us, event | category | flops | bytes accessed | tf_op | source)
XLA Modules:
  0.0 304.3 jit_solution(11180192331451600958)
XLA Ops:
  1.8 2.6 pack_attn.1
  4.4 2.9 collective-permute-start
  8.0 3.5 %pack_ffn.1 = (bf16[400,768]{1,0:T(8,128)(2,1)}, bf16[384,768]{1,0:T(8,128)(2,1)}, bf16[2,512,128]{2,1,0:T(8,128)(2,1)}, bf16[2,512,128]{2,1,0:T(8,128)(2,1)}) custom-call(s32[13]{0:T(128)} %or_select_fusion.info_ref.refs_0_.at_ref, s32[4,4]{1,0:T(4,128)} %seg_ref.1, bf16[768,1536]{1,0:T(8,128)(2,1)} %wu_m_ref.1, bf16[1536,768]{1,0:T(8,128)(2,1)} %wd_m_ref.1, ...), custom_call_target="tpu_custom_call" | custom-call | bytes 33554432 | tf_op jit(solution)/shard_map/pack_ffn/pallas_call | solution.py:484
  13.5 8.7 %attn_fwd.3 = (bf16[3,1024,384]{2,1,0:T(8,128)(2,1)}, bf16[1024,384]{1,0:T(8,128)(2,1)S(1)}, bf16[12,512,512]{2,1,0:T(8,128)(2,1)}, f32[2,3,2,512]{3,2,1,0:T(2,128)S(1)}) custom-call(s32[13]{0:T(128)S(1)} %copy-done.19, s32[4]{0:T(128)S(1)} %copy-done.27, bf16[1024,768]{1,0:T(8,128)(2,1)S(1)} %copy-done.1, bf16[3,768,384]{2,1,0:T(8,128)(2,1)S(1)} %copy-done, ...), custom_call_target="tpu_custom_call" | custom-call | flops 800000 | bytes 8000 | tf_op jit(solution)/shard_map/attn_fwd/pallas_call | solution.py:86
  24.5 5.1 %attn_fwd.4 = (bf16[3,1024,384]{2,1,0:T(8,128)(2,1)}, bf16[1024,384]{1,0:T(8,128)(2,1)S(1)}, bf16[12,512,512]{2,1,0:T(8,128)(2,1)}, f32[2,3,2,512]{3,2,1,0:T(2,128)S(1)}) custom-call(s32[13]{0:T(128)S(1)} %copy-done.19, s32[4]{0:T(128)S(1)} %copy-done.27, ...), custom_call_target="tpu_custom_call", output_to_operand_aliasing={{0}: (7, {}), {1}: (8, {}), {2}: (9, {}), {3}: (10, {})} | custom-call | flops 800000 | bytes 8000 | tf_op jit(solution)/shard_map/attn_fwd/pallas_call | solution.py:86
  31.1 3.6 %collective-permute-done.3.refs_0_ = bf16[400,768]{1,0:T(8,128)(2,1)} collective-permute-done((bf16[400,768]{1,0:T(8,128)(2,1)}, bf16[400,768]{1,0:T(8,128)(2,1)}, u32[]{:S(2)}, u32[]{:S(2)}) %collective-permute-start.3) | collective-permute-done | bytes 614432 | tf_op jit(solution)/shard_map/ppermute | solution.py:544
  35.5 3.8 %collective-permute-done.1.refs_1_ = bf16[400,768]{1,0:T(8,128)(2,1)} collective-permute-done((bf16[400,768]{1,0:T(8,128)(2,1)}, bf16[400,768]{1,0:T(8,128)(2,1)}, u32[]{:S(2)}, u32[]{:S(2)}) %collective-permute-start.1) | collective-permute-done | bytes 614432 | tf_op jit(solution)/shard_map/ppermute | solution.py:549
  45.6 12.3 %attn_fwd.5 = (bf16[3,1024,384]{2,1,0:T(8,128)(2,1)}, bf16[1024,384]{1,0:T(8,128)(2,1)S(1)}, bf16[12,512,512]{2,1,0:T(8,128)(2,1)}, f32[2,3,2,512]{3,2,1,0:T(2,128)S(1)}) custom-call(s32[13]{0:T(128)S(1)} %copy-done.19, s32[4]{0:T(128)S(1)} %copy-done.27, bf16[1024,768]{1,0:T(8,128)(2,1)S(1)} %copy-done.1, ...), custom_call_target="tpu_custom_call" | custom-call | flops 800000 | bytes 8000 | tf_op jit(solution)/shard_map/attn_fwd/pallas_call | solution.py:86
  60.1 15.0 %ffn_front.1 = (bf16[1024,768]{1,0:T(8,128)(2,1)S(1)}, f32[1024,768]{1,0:T(8,128)}, f32[1024,1]{1,0:T(8,128)S(1)}, f32[1024,768]{1,0:T(8,128)}, bf16[2,1024,768]...) custom-call(s32[13]{0:T(128)S(1)} %copy-done.19, bf16[1024,384]{1,0:T(8,128)(2,1)S(1)} %copy-done.13, ...), custom_call_target="tpu_custom_call" | custom-call | flops 80000000000 | bytes 150994944 | tf_op jit(solution)/shard_map/ffn_front/pallas_call | solution.py:304
  80.4 39.0 %ffn_back.1 = (bf16[1024,768]{1,0:T(8,128)(2,1)}, f32[2,768]{1,0:T(2,128)}, bf16[2,1024,768]{2,1,0:T(8,128)(2,1)}, bf16[1024,768]{1,0:T(8,128)(2,1)S(1)}, bf16[2...) custom-call(s32[13]{0:T(128)S(1)} %copy-done.19, ...), custom_call_target="tpu_custom_call" | custom-call | flops 199999995904 | bytes 251658240 | tf_op jit(solution)/shard_map/ffn_back/pallas_call | solution.py:391
  119.4 2.6 slice_bitcast_fusion.2
  136.3 2.5 fusion.19
  140.9 2.7 fusion.22
  143.7 16.8 %attn_bwd.2 = (bf16[3,1024,384]{2,1,0:T(8,128)(2,1)}, bf16[2,384,768]{2,1,0:T(8,128)(2,1)}, bf16[2,384,768]{2,1,0:T(8,128)(2,1)}, f32[2,384]{1,0:T(2,128)S(1)}) custom-call(s32[13]{0:T(128)S(1)} %copy-done.19, bf16[1024,768]{1,0:T(8,128)(2,1)S(1)} %copy-done.2, bf16[1024,768]{1,0:T(8,128)(2,1)S(1)} %get-tuple-element.194.ga_ref, ...), custom_call_target="tpu_custom_call" | custom-call | flops 128000000000 | bytes 50331648 | tf_op jit(solution)/shard_map/attn_bwd/pallas_call | solution.py:191
  164.5 3.1 %add_convert_fusion.4 = bf16[768,768]{1,0:T(8,128)(2,1)} fusion(bf16[768,768]{1,0:T(8,128)(2,1)} %collective-permute-done.15, bf16[768,768]{1,0:T(8,128)(2,1)} %fusion.22), kind=kLoop, calls=%fused_computation.7 | loop fusion | flops 2359296 | bytes 3538944 | tf_op jit(solution)/shard_map/convert_element_type | solution.py:620
  174.5 17.1 %attn_bwd.3 = (bf16[3,1024,384]{2,1,0:T(8,128)(2,1)}, bf16[2,384,768]{2,1,0:T(8,128)(2,1)}, bf16[2,384,768]{2,1,0:T(8,128)(2,1)}, f32[2,384]{1,0:T(2,128)S(1)}) custom-call(s32[13]{0:T(128)S(1)} %copy-done.19, bf16[1024,768]{1,0:T(8,128)(2,1)S(1)} %copy-done.2, bf16[1024,768]{1,0:T(8,128)(2,1)S(1)} %copy-done.36, bf16[384,768]{1,0:T(8,128)(2,1)S(1)} %copy-done.18, ...), custom_call_target="tpu_custom_call" | custom-call | flops 128000000000 | bytes 50331648 | tf_op jit(solution)/shard_map/attn_bwd/pallas_call | solution.py:191
  209.3 2.7 collective-permute-start.26
  212.0 6.5 %collective-permute-done.23 = f32[16,768]{1,0:T(8,128)S(1)} collective-permute-done((f32[16,768]{1,0:T(8,128)S(1)}, f32[16,768]{1,0:T(8,128)S(1)}, u32[]{:S(2)}, u32[]{:S(2)}) %collective-permute-start.23) | collective-permute-done | bytes 49184 | tf_op jit(solution)/shard_map/ppermute | solution.py:544
  218.6 4.1 %collective-permute-done.24 = bf16[384,768]{1,0:T(8,128)(2,1)S(1)} collective-permute-done((bf16[384,768]{1,0:T(8,128)(2,1)S(1)}, bf16[384,768]{1,0:T(8,128)(2,1)S(1)}, u32[]{:S(2)}, u32[]{:S(2)}) %collective-permute-start.24) | collective-permute-done | bytes 589856 | tf_op jit(solution)/shard_map/ppermute | solution.py:549
  226.4 2.4 collective-permute-start.31
  234.2 5.9 %collective-permute-done.31 = bf16[192,768]{1,0:T(8,128)(2,1)S(1)} collective-permute-done((bf16[192,768]{1,0:T(8,128)(2,1)S(1)}, bf16[192,768]{1,0:T(8,128)(2,1)S(1)}, u32[]{:S(2)}, u32[]{:S(2)}) %collective-permute-start.31) | collective-permute-done | bytes 294944 | tf_op jit(solution)/shard_map/ppermute | solution.py:549
  243.7 3.1 %collective-permute-start.38 = (bf16[96,768]{1,0:T(8,128)(2,1)S(1)}, bf16[96,768]{1,0:T(8,128)(2,1)S(1)}, u32[]{:S(2)}, u32[]{:S(2)}) collective-permute-start(bf16[96,768]{1,0:T(8,128)(2,1)S(1)} %add_convert_fusion.17.refs_0_), channel_id=1, source_target_pairs={{0,16},{2,18},{4,20},{6,22},{8,24},{10,26},{12,28},{14,30},{16,0},... | collective-permute-start | bytes 442376 | tf_op jit(solution)/shard_map/ppermute | solution.py:549
  249.0 10.3 %collective-permute-done.38.refs_1_ = bf16[96,768]{1,0:T(8,128)(2,1)S(1)} collective-permute-done((bf16[96,768]{1,0:T(8,128)(2,1)S(1)}, bf16[96,768]{1,0:T(8,128)(2,1)S(1)}, u32[]{:S(2)}, u32[]{:S(2)}) %collective-permute-start.38) | collective-permute-done | bytes 147488 | tf_op jit(solution)/shard_map/ppermute | solution.py:549
  261.1 2.7 collective-permute-start.39
  265.9 2.8 collective-permute-start.41
  271.1 2.2 fusion.37
  273.7 3.4 %fusion = bf16[1024,768]{1,0:T(8,128)(2,1)} fusion(f32[1024,768]{1,0:T(8,128)S(1)} %copy-done.56, f32[1024,768,1]{1,0,2:T(8,128)S(1)} %fusion.37, bf16[3,1024,384]{2,1,0:T(8,128)(2,1)S(1)} %copy-done.57, bf16[3,768,384]{2,1,0:T(8,128)(2,1)S(1)} %copy-done), kind=kOutput, calls=%fused_computation.1 | convolution fusion | flops 1814298624 | bytes 11993088 | tf_op jit(solution)/shard_map/cte,cde->td/dot_general | solution.py:803
  279.0 3.0 place_kernel.1
  282.0 6.1 %collective-permute-done.45.refs_3_ = bf16[384,768]{1,0:T(8,128)(2,1)S(1)} collective-permute-done((bf16[384,768]{1,0:T(8,128)(2,1)S(1)}, bf16[384,768]{1,0:T(8,128)(2,1)S(1)}, u32[]{:S(2)}, u32[]{:S(2)}) %collective-permute-start.45) | collective-permute-done | bytes 589856 | tf_op jit(solution)/shard_map/ppermute | solution.py:549
  289.2 3.2 %collective-permute-done.43.refs_3_ = bf16[384,768]{1,0:T(8,128)(2,1)S(1)} collective-permute-done((bf16[384,768]{1,0:T(8,128)(2,1)S(1)}, bf16[384,768]{1,0:T(8,128)(2,1)S(1)}, u32[]{:S(2)}, u32[]{:S(2)}) %collective-permute-start.43) | collective-permute-done | bytes 589856 | tf_op jit(solution)/shard_map/ppermute | solution.py:549
  296.1 3.0 %place_up_kernel.1 = f32[768,1536]{1,0:T(8,128)} custom-call(s32[16]{0:T(128)S(1)} %fusion.34.at_ref, bf16[96,768]{1,0:T(8,128)(2,1)S(1)} %add_convert_fusion.17.refs_0_, bf16[96,768]{1,0:T(8,128)(2,1)S(1)} %collective-permute-done.38.refs_1_, bf16[192,768]{1,0:T(8,128)(2,1)S(1)} %collective-permute-done.40.refs_2_, ...), custom_call_target="tpu_custom_call" | custom-call | bytes 56623104 | tf_op jit(solution)/shard_map/place_up_kernel/pallas_call | solution.py:600
  299.1 4.7 %place_attn_kernel.1 = (f32[3,768,384]{2,1,0:T(8,128)}, f32[384,768]{1,0:T(8,128)}) custom-call(s32[16]{0:T(128)S(1)} %fusion.35.at_ref, bf16[96,768]{1,0:T(8,128)(2,1)S(1)} %add_convert_fusion.16.refs_0_, bf16[96,768]{1,0:T(8,128)(2,1)S(1)} %collective-permute-done.36.refs_1_, bf16[192,768]{1,0:T(8,128)(2,1)S(1)} %collective-permute-done.42.refs_2_, ...), custom_call_target="tpu_custom_call" | custom-call | bytes 56623104 | tf_op jit(solution)/shard_map/place_attn_kernel/pallas_call | solution.py:600
  (272 shorter events, 89.5 us)
Async XLA Ops:
  4.4 17.9 %collective-permute-start = (bf16[400,768]{1,0:T(8,128)(2,1)}, bf16[400,768]{1,0:T(8,128)(2,1)}, u32[]{:S(2)}, u32[]{:S(2)}) collective-permute-start(bf16[400,768]{1,0:T(8,128)(2,1)} %pack_attn.1), channel_id=1, source_target_pairs={{0,1},{1,0},{2,3},{3,2},{4,5},{5,4},{6,7},{7,6},{8,9},{9,8},{10,11... | collective-permute-start | bytes 1843208 | tf_op jit(solution)/shard_map/ppermute | solution.py:544
  11.5 23.2 %collective-permute-start.3 = (bf16[400,768]{1,0:T(8,128)(2,1)}, bf16[400,768]{1,0:T(8,128)(2,1)}, u32[]{:S(2)}, u32[]{:S(2)}) collective-permute-start(bf16[400,768]{1,0:T(8,128)(2,1)} %get-tuple-element.138), channel_id=1, source_target_pairs={{0,1},{1,0},{2,3},{3,2},{4,5},{5,4},{6,7},{7,6},{8,9},{9,8},{10,11... | collective-permute-start | bytes 1843208 | tf_op jit(solution)/shard_map/ppermute | solution.py:544
  22.4 12.3 %collective-permute-start.2 = (bf16[400,768]{1,0:T(8,128)(2,1)}, bf16[400,768]{1,0:T(8,128)(2,1)S(1)}, u32[]{:S(2)}, u32[]{:S(2)}) collective-permute-start(bf16[400,768]{1,0:T(8,128)(2,1)} %collective-permute-done.refs_0_), channel_id=1, source_target_pairs={{0,2},{2,0},{4,6},{6,4},{8,10},{10,8},{12,14},{14,12},{16,18},{18,... | collective-permute-start | bytes 1843208 | tf_op jit(solution)/shard_map/ppermute | solution.py:549
  22.4 16.9 %collective-permute-start.1 = (bf16[400,768]{1,0:T(8,128)(2,1)}, bf16[400,768]{1,0:T(8,128)(2,1)}, u32[]{:S(2)}, u32[]{:S(2)}) collective-permute-start(bf16[400,768]{1,0:T(8,128)(2,1)} %collective-permute-done.refs_0_), channel_id=1, source_target_pairs={{0,4},{2,6},{4,0},{6,2},{8,12},{10,14},{12,8},{14,10},{16,20},{18,... | collective-permute-start | bytes 1843208 | tf_op jit(solution)/shard_map/ppermute | solution.py:549
  39.3 18.5 %collective-permute-start.6 = (bf16[400,768]{1,0:T(8,128)(2,1)}, bf16[400,768]{1,0:T(8,128)(2,1)}, u32[]{:S(2)}, u32[]{:S(2)}) collective-permute-start(bf16[400,768]{1,0:T(8,128)(2,1)} %collective-permute-done.3.refs_0_), channel_id=1, source_target_pairs={{0,4},{2,6},{4,0},{6,2},{8,12},{10,14},{12,8},{14,10},{16,20},{18,... | collective-permute-start | bytes 1843208 | tf_op jit(solution)/shard_map/ppermute | solution.py:549
  41.0 16.8 %collective-permute-start.5 = (bf16[384,768]{1,0:T(8,128)(2,1)}, bf16[384,768]{1,0:T(8,128)(2,1)}, u32[]{:S(2)}, u32[]{:S(2)}) collective-permute-start(bf16[384,768]{1,0:T(8,128)(2,1)} %get-tuple-element.145), channel_id=1, source_target_pairs={{0,1},{1,0},{2,3},{3,2},{4,5},{5,4},{6,7},{7,6},{8,9},{9,8},{10,11... | collective-permute-start | bytes 1769480 | tf_op jit(solution)/shard_map/ppermute | solution.py:544
  57.9 17.2 %collective-permute-start.10 = (bf16[384,768]{1,0:T(8,128)(2,1)}, bf16[384,768]{1,0:T(8,128)(2,1)S(1)}, u32[]{:S(2)}, u32[]{:S(2)}) collective-permute-start(bf16[384,768]{1,0:T(8,128)(2,1)} %collective-permute-done.5.refs_4_), channel_id=1, source_target_pairs={{0,2},{2,0},{4,6},{6,4},{8,10},{10,8},{12,14},{14,12},{16,18},{18,... | collective-permute-start | bytes 1769480 | tf_op jit(solution)/shard_map/ppermute | solution.py:549
  57.9 17.1 %collective-permute-start.7 = (bf16[384,768]{1,0:T(8,128)(2,1)}, bf16[384,768]{1,0:T(8,128)(2,1)S(1)}, u32[]{:S(2)}, u32[]{:S(2)}) collective-permute-start(bf16[384,768]{1,0:T(8,128)(2,1)} %collective-permute-done.5.refs_4_), channel_id=1, source_target_pairs={{0,8},{2,10},{4,12},{6,14},{8,0},{10,2},{12,4},{14,6},{16,24},{18,... | collective-permute-start | bytes 1769480 | tf_op jit(solution)/shard_map/ppermute | solution.py:549
  59.6 15.5 %collective-permute-start.8 = (bf16[400,768]{1,0:T(8,128)(2,1)}, bf16[400,768]{1,0:T(8,128)(2,1)S(1)}, u32[]{:S(2)}, u32[]{:S(2)}) collective-permute-start(bf16[400,768]{1,0:T(8,128)(2,1)} %collective-permute-done.3.refs_0_), channel_id=1, source_target_pairs={{0,2},{2,0},{4,6},{6,4},{8,10},{10,8},{12,14},{14,12},{16,18},{18,... | collective-permute-start | bytes 1843208 | tf_op jit(solution)/shard_map/ppermute | solution.py:549
  59.7 15.4 %collective-permute-start.9 = (bf16[400,768]{1,0:T(8,128)(2,1)}, bf16[400,768]{1,0:T(8,128)(2,1)S(1)}, u32[]{:S(2)}, u32[]{:S(2)}) collective-permute-start(bf16[400,768]{1,0:T(8,128)(2,1)} %collective-permute-done.6.refs_1_), channel_id=1, source_target_pairs={{0,2},{2,0},{4,6},{6,4},{8,10},{10,8},{12,14},{14,12},{16,18},{18,... | collective-permute-start | bytes 1843208 | tf_op jit(solution)/shard_map/ppermute | solution.py:549
  138.7 25.7 %collective-permute-start.15 = (bf16[768,768]{1,0:T(8,128)(2,1)}, bf16[768,768]{1,0:T(8,128)(2,1)}, u32[]{:S(2)}, u32[]{:S(2)}) collective-permute-start(bf16[768,768]{1,0:T(8,128)(2,1)} %fusion.19), channel_id=1, source_target_pairs={{0,2},{2,0},{4,6},{6,4},{8,10},{10,8},{12,14},{14,12},{16,18},{18,... | collective-permute-start | bytes 3538952 | tf_op jit(solution)/shard_map/ppermute | solution.py:549
  138.9 29.1 %collective-permute-start.16 = (bf16[768,768]{1,0:T(8,128)(2,1)}, bf16[768,768]{1,0:T(8,128)(2,1)}, u32[]{:S(2)}, u32[]{:S(2)}) collective-permute-start(bf16[768,768]{1,0:T(8,128)(2,1)} %add_convert_fusion.7), channel_id=1, source_target_pairs={{0,1},{1,0},{2,3},{3,2},{4,5},{5,4},{6,7},{7,6},{8,9},{9,8},{10,11... | collective-permute-start | bytes 3538952 | tf_op jit(solution)/shard_map/ppermute | solution.py:544
  161.1 10.0 %collective-permute-start.17 = (bf16[768,768]{1,0:T(8,128)(2,1)}, bf16[768,768]{1,0:T(8,128)(2,1)}, u32[]{:S(2)}, u32[]{:S(2)}) collective-permute-start(bf16[768,768]{1,0:T(8,128)(2,1)} %bitcast.69), channel_id=1, source_target_pairs={{0,2},{2,0},{4,6},{6,4},{8,10},{10,8},{12,14},{14,12},{16,18},{18,... | collective-permute-start | bytes 3538952 | tf_op jit(solution)/shard_map/ppermute | solution.py:549
  163.0 39.5 %collective-permute-start.20 = (bf16[768,768]{1,0:T(8,128)(2,1)}, bf16[768,768]{1,0:T(8,128)(2,1)}, u32[]{:S(2)}, u32[]{:S(2)}) collective-permute-start(bf16[768,768]{1,0:T(8,128)(2,1)} %add_convert_fusion.5), channel_id=1, source_target_pairs={{0,1},{1,0},{2,3},{3,2},{4,5},{5,4},{6,7},{7,6},{8,9},{9,8},{10,11... | collective-permute-start | bytes 3538952 | tf_op jit(solution)/shard_map/ppermute | solution.py:544
  170.5 27.1 %collective-permute-start.18 = (bf16[384,768]{1,0:T(8,128)(2,1)}, bf16[384,768]{1,0:T(8,128)(2,1)}, u32[]{:S(2)}, u32[]{:S(2)}) collective-permute-start(bf16[384,768]{1,0:T(8,128)(2,1)} %constant_dynamic-slice_fusion.9), channel_id=1, source_target_pairs={{0,8},{2,10},{4,12},{6,14},{8,0},{10,2},{12,4},{14,6},{16,24},{18,... | collective-permute-start | bytes 1769480 | tf_op jit(solution)/shard_map/ppermute | solution.py:549
  174.1 26.7 %collective-permute-start.19 = (bf16[384,768]{1,0:T(8,128)(2,1)}, bf16[384,768]{1,0:T(8,128)(2,1)}, u32[]{:S(2)}, u32[]{:S(2)}) collective-permute-start(bf16[384,768]{1,0:T(8,128)(2,1)} %constant_dynamic-slice_fusion.8), channel_id=1, source_target_pairs={{0,4},{2,6},{4,0},{6,2},{8,12},{10,14},{12,8},{14,10},{16,20},{18,... | collective-permute-start | bytes 1769480 | tf_op jit(solution)/shard_map/ppermute | solution.py:549
  192.1 13.2 %collective-permute-start.21 = (bf16[768,768]{1,0:T(8,128)(2,1)}, bf16[768,768]{1,0:T(8,128)(2,1)}, u32[]{:S(2)}, u32[]{:S(2)}) collective-permute-start(bf16[768,768]{1,0:T(8,128)(2,1)} %bitcast.68), channel_id=1, source_target_pairs={{0,2},{2,0},{4,6},{6,4},{8,10},{10,8},{12,14},{14,12},{16,18},{18,... | collective-permute-start | bytes 3538952 | tf_op jit(solution)/shard_map/ppermute | solution.py:549
  199.0 10.2 %collective-permute-start.22 = (bf16[192,768]{1,0:T(8,128)(2,1)S(1)}, bf16[192,768]{1,0:T(8,128)(2,1)S(1)}, u32[]{:S(2)}, u32[]{:S(2)}) collective-permute-start(bf16[192,768]{1,0:T(8,128)(2,1)S(1)} %constant_dynamic-slice_fusion.7), channel_id=1, source_target_pairs={{0,4},{2,6},{4,0},{6,2},{8,12},{10,14},{12,8},{14,10},{16,20},{18,... | collective-permute-start | bytes 884744 | tf_op jit(solution)/shard_map/ppermute | solution.py:549
  202.0 22.8 %collective-permute-start.28 = (bf16[384,768]{1,0:T(8,128)(2,1)S(1)}, bf16[384,768]{1,0:T(8,128)(2,1)S(1)}, u32[]{:S(2)}, u32[]{:S(2)}) collective-permute-start(bf16[384,768]{1,0:T(8,128)(2,1)S(1)} %add_convert_fusion.11), channel_id=1, source_target_pairs={{0,1},{1,0},{2,3},{3,2},{4,5},{5,4},{6,7},{7,6},{8,9},{9,8},{10,11... | collective-permute-start | bytes 1769480 | tf_op jit(solution)/shard_map/ppermute | solution.py:544
  204.2 18.5 %collective-permute-start.24 = (bf16[384,768]{1,0:T(8,128)(2,1)S(1)}, bf16[384,768]{1,0:T(8,128)(2,1)S(1)}, u32[]{:S(2)}, u32[]{:S(2)}) collective-permute-start(bf16[384,768]{1,0:T(8,128)(2,1)S(1)} %constant_dynamic-slice_fusion.6), channel_id=1, source_target_pairs={{0,8},{2,10},{4,12},{6,14},{8,0},{10,2},{12,4},{14,6},{16,24},{18,... | collective-permute-start | bytes 1769480 | tf_op jit(solution)/shard_map/ppermute | solution.py:549
  207.0 11.5 %collective-permute-start.23 = (f32[16,768]{1,0:T(8,128)S(1)}, f32[16,768]{1,0:T(8,128)S(1)}, u32[]{:S(2)}, u32[]{:S(2)}) collective-permute-start(f32[16,768]{1,0:T(8,128)S(1)} %copy-done.53), channel_id=1, source_target_pairs={{0,1},{1,0},{2,3},{3,2},{4,5},{5,4},{6,7},{7,6},{8,9},{9,8},{10,11... | collective-permute-start | bytes 147464 | tf_op jit(solution)/shard_map/ppermute | solution.py:544
  208.7 15.8 %collective-permute-start.25 = (bf16[384,768]{1,0:T(8,128)(2,1)S(1)}, bf16[384,768]{1,0:T(8,128)(2,1)S(1)}, u32[]{:S(2)}, u32[]{:S(2)}) collective-permute-start(bf16[384,768]{1,0:T(8,128)(2,1)S(1)} %constant_dynamic-slice_fusion.5), channel_id=1, source_target_pairs={{0,4},{2,6},{4,0},{6,2},{8,12},{10,14},{12,8},{14,10},{16,20},{18,... | collective-permute-start | bytes 1769480 | tf_op jit(solution)/shard_map/ppermute | solution.py:549
  209.3 15.4 %collective-permute-start.26 = (bf16[96,768]{1,0:T(8,128)(2,1)S(1)}, bf16[96,768]{1,0:T(8,128)(2,1)S(1)}, u32[]{:S(2)}, u32[]{:S(2)}) collective-permute-start(bf16[96,768]{1,0:T(8,128)(2,1)S(1)} %constant_dynamic-slice_fusion.4), channel_id=1, source_target_pairs={{0,16},{2,18},{4,20},{6,22},{8,24},{10,26},{12,28},{14,30},{16,0},... | collective-permute-start | bytes 442376 | tf_op jit(solution)/shard_map/ppermute | solution.py:549
  218.5 15.7 %collective-permute-start.30 = (f32[16,768]{1,0:T(8,128)S(1)}, f32[16,768]{1,0:T(8,128)S(1)}, u32[]{:S(2)}, u32[]{:S(2)}) collective-permute-start(f32[16,768]{1,0:T(8,128)S(1)} %add.176), channel_id=1, source_target_pairs={{0,2},{2,0},{4,6},{6,4},{8,10},{10,8},{12,14},{14,12},{16,18},{18,... | collective-permute-start | bytes 147464 | tf_op jit(solution)/shard_map/ppermute | solution.py:549
  226.4 13.8 %collective-permute-start.31 = (bf16[192,768]{1,0:T(8,128)(2,1)S(1)}, bf16[192,768]{1,0:T(8,128)(2,1)S(1)}, u32[]{:S(2)}, u32[]{:S(2)}) collective-permute-start(bf16[192,768]{1,0:T(8,128)(2,1)S(1)} %constant_dynamic-slice_fusion.2), channel_id=1, source_target_pairs={{0,8},{2,10},{4,12},{6,14},{8,0},{10,2},{12,4},{14,6},{16,24},{18,... | collective-permute-start | bytes 884744 | tf_op jit(solution)/shard_map/ppermute | solution.py:549
  241.8 23.0 %collective-permute-start.37 = (bf16[384,768]{1,0:T(8,128)(2,1)S(1)}, bf16[384,768]{1,0:T(8,128)(2,1)S(1)}, u32[]{:S(2)}, u32[]{:S(2)}) collective-permute-start(bf16[384,768]{1,0:T(8,128)(2,1)S(1)} %pad_maximum_fusion.3), channel_id=1, source_target_pairs={{0,8},{2,10},{4,12},{6,14},{8,0},{10,2},{12,4},{14,6},{16,24},{18,... | collective-permute-start | bytes 1769480 | tf_op jit(solution)/shard_map/ppermute | solution.py:549
  243.7 15.6 %collective-permute-start.38 = (bf16[96,768]{1,0:T(8,128)(2,1)S(1)}, bf16[96,768]{1,0:T(8,128)(2,1)S(1)}, u32[]{:S(2)}, u32[]{:S(2)}) collective-permute-start(bf16[96,768]{1,0:T(8,128)(2,1)S(1)} %add_convert_fusion.17.refs_0_), channel_id=1, source_target_pairs={{0,16},{2,18},{4,20},{6,22},{8,24},{10,26},{12,28},{14,30},{16,0},... | collective-permute-start | bytes 442376 | tf_op jit(solution)/shard_map/ppermute | solution.py:549
  248.9 14.9 %collective-permute-start.36 = (bf16[96,768]{1,0:T(8,128)(2,1)S(1)}, bf16[96,768]{1,0:T(8,128)(2,1)S(1)}, u32[]{:S(2)}, u32[]{:S(2)}) collective-permute-start(bf16[96,768]{1,0:T(8,128)(2,1)S(1)} %add_convert_fusion.16.refs_0_), channel_id=1, source_target_pairs={{0,16},{2,18},{4,20},{6,22},{8,24},{10,26},{12,28},{14,30},{16,0},... | collective-permute-start | bytes 442376 | tf_op jit(solution)/shard_map/ppermute | solution.py:549
  268.7 9.6 %collective-permute-start.42 = (bf16[192,768]{1,0:T(8,128)(2,1)S(1)}, bf16[192,768]{1,0:T(8,128)(2,1)S(1)}, u32[]{:S(2)}, u32[]{:S(2)}) collective-permute-start(bf16[192,768]{1,0:T(8,128)(2,1)S(1)} %pad_maximum_fusion.7), channel_id=1, source_target_pairs={{0,8},{2,10},{4,12},{6,14},{8,0},{10,2},{12,4},{14,6},{16,24},{18,... | collective-permute-start | bytes 884744 | tf_op jit(solution)/shard_map/ppermute | solution.py:549
  269.7 9.3 %collective-permute-start.44 = (bf16[768,768]{1,0:T(8,128)(2,1)S(1)}, bf16[768,768]{1,0:T(8,128)(2,1)S(1)}, u32[]{:S(2)}, u32[]{:S(2)}) collective-permute-start(bf16[768,768]{1,0:T(8,128)(2,1)S(1)} %pad_maximum_fusion), channel_id=1, source_target_pairs={{0,2},{2,0},{4,6},{6,4},{8,10},{10,8},{12,14},{14,12},{16,18},{18,... | collective-permute-start | bytes 3538952 | tf_op jit(solution)/shard_map/ppermute | solution.py:549
  269.7 18.4 %collective-permute-start.45 = (bf16[384,768]{1,0:T(8,128)(2,1)S(1)}, bf16[384,768]{1,0:T(8,128)(2,1)S(1)}, u32[]{:S(2)}, u32[]{:S(2)}) collective-permute-start(bf16[384,768]{1,0:T(8,128)(2,1)S(1)} %pad_maximum_fusion.4), channel_id=1, source_target_pairs={{0,8},{2,10},{4,12},{6,14},{8,0},{10,2},{12,4},{14,6},{16,24},{18,... | collective-permute-start | bytes 1769480 | tf_op jit(solution)/shard_map/ppermute | solution.py:549
  278.3 14.1 %collective-permute-start.43 = (bf16[384,768]{1,0:T(8,128)(2,1)S(1)}, bf16[384,768]{1,0:T(8,128)(2,1)S(1)}, u32[]{:S(2)}, u32[]{:S(2)}) collective-permute-start(bf16[384,768]{1,0:T(8,128)(2,1)S(1)} %pad_maximum_fusion.5), channel_id=1, source_target_pairs={{0,4},{2,6},{4,0},{6,2},{8,12},{10,14},{12,8},{14,10},{16,20},{18,... | collective-permute-start | bytes 1769480 | tf_op jit(solution)/shard_map/ppermute | solution.py:549
  (77 other events, 494.1 us)
